TPU v7x, 256 devices: a whole 4x4x8 slice. The times are simulated.
256 devices in a mesh: dp: 16 (over x, z_lo, core), sh: 4 (over z_hi), sw: 4 (over y).
Axes of the slice: x: 4, y: 4, z: 8 (z_hi: 4, z_lo: 2; z = z_hi * 2 + z_lo), core: 2. Of those that a mesh axis runs over, the one named last changes fastest.
Arguments:
- query_tokens: bfloat16 [16, 2, 32, 32, 1536], P('dp', None, 'sh', 'sw'), may hold values from -18 to 18
- key_tokens: bfloat16 [16, 2, 32, 32, 1536], P('dp', None, 'sh', 'sw'), may hold values from -18 to 18
- value_tokens: bfloat16 [16, 2, 32, 32, 1536], P('dp', None, 'sh', 'sw'), may hold values from -24 to 24
- window_first_tile: int32 [2, 4, 4], replicated, may hold values from 0 to 1, as said below
- output_weight_matrix: bfloat16 [1536, 1536], P(None, 'dp'), may hold values from -0.15625 to 0.15625
- adapter_down_weight: bfloat16 [1536, 64], replicated, may hold values from -0.15625 to 0.15625
- adapter_up_weight: bfloat16 [64, 1536], replicated, may hold values from -0.75 to 0.75
- output_gradient: bfloat16 [16, 2, 32, 32, 1536], P('dp', None, 'sh', 'sw'), may hold values from -6 to 6
Outputs:
- output: bfloat16 [16, 2, 32, 32, 1536], P('dp', None, 'sh', 'sw')
- query_grad: bfloat16 [16, 2, 32, 32, 1536], P('dp', None, 'sh', 'sw')
- key_grad: bfloat16 [16, 2, 32, 32, 1536], P('dp', None, 'sh', 'sw')
- value_grad: bfloat16 [16, 2, 32, 32, 1536], P('dp', None, 'sh', 'sw')
- down_grad: float32 [1536, 64], replicated
- up_weight_gradient: float32 [64, 1536], replicated
Inputs may be any that keep to these rules, and one draw needn't show every extreme that they name: window_first_tile[0, i, j] lies between max(0, i - 2) and min(i, 1); window_first_tile[1, i, j] between max(0, j - 2) and min(j, 1).
All inputs are finite; a program needn't handle non-finite values.
Results may differ from a plain program's by a relative error of at most 0.024.
Values may be sent and summed in bfloat16 or wider, within the bound.
A program may use at most 128 MiB of HBM per device.

v0:
```python
import jax
import jax.numpy as jnp
from jax import lax
from jax.sharding import PartitionSpec as P

HEADS = 12
WINDOW = 3


def table_entry(window_first_tile, which, row_index, col_index):
    return lax.dynamic_slice(window_first_tile, (which, row_index, col_index), (1, 1, 1))[0, 0, 0]


def body(
    query_tokens,
    key_tokens,
    value_tokens,
    window_first_tile,
    output_weight_matrix,
    adapter_down_weight,
    adapter_up_weight,
    output_gradient,
):
    rows_axis = lax.axis_size("sh")
    cols_axis = lax.axis_size("sw")
    samples, frames, tile_rows, tile_cols, channels = query_tokens.shape
    head_dim = channels // HEADS
    per_group = 2
    group_count = HEADS // per_group
    group_span = per_group * head_dim
    factor = head_dim ** (-0.5)
    my_row = lax.axis_index("sh")
    my_col = lax.axis_index("sw")
    row_begin = table_entry(window_first_tile, 0, my_row, my_col)
    col_begin = table_entry(window_first_tile, 1, my_row, my_col)
    tile_tokens = frames * tile_rows * tile_cols
    contract_trailing = (((1,), (1,)), ((), ()))
    contract_leading = (((0,), (0,)), ((), ()))
    gathered = (
        lax.all_gather(key_tokens[None], ("sh", "sw"), axis=0, tiled=True),
        lax.all_gather(value_tokens[None], ("sh", "sw"), axis=0, tiled=True),
    )
    grid_shape = (rows_axis, cols_axis) + key_tokens.shape

    def windowed(block):
        return lax.dynamic_slice(
            block.reshape(grid_shape),
            (row_begin, col_begin, 0, 0, 0, 0, 0),
            (WINDOW, WINDOW) + key_tokens.shape,
        )

    key_window = windowed(gathered[0])
    value_window = windowed(gathered[1])

    def heads_of(array, head_group):
        return array[..., head_group * group_span : (head_group + 1) * group_span].reshape(
            -1, per_group, head_dim
        )

    row_tops = []
    row_totals = []
    sample = 0
    top_list = []
    total_list = []
    weight_list = []
    pieces_out = []
    for head_group in range(group_count):
        query_heads = heads_of(query_tokens[sample], head_group)
        key_heads = heads_of(key_window[:, :, sample], head_group)
        value_heads = heads_of(value_window[:, :, sample], head_group)
        scores = (
            jnp.einsum("qhd,khd->hqk", query_heads, key_heads, preferred_element_type=jnp.float32)
            * factor
        )
        row_top = jnp.max(scores, axis=-1)
        exponent = jnp.exp(scores - row_top[..., None])
        row_total = jnp.sum(exponent, axis=-1)
        weights = (exponent / row_total[..., None]).astype(jnp.bfloat16)
        top_list.append(row_top)
        total_list.append(row_total)
        weight_list.append(weights)
        attended_part = jnp.einsum(
            "hqk,khd->qhd", weights, value_heads, preferred_element_type=jnp.float32
        )
        pieces_out.append(attended_part.astype(jnp.bfloat16).reshape(tile_tokens, group_span))
    row_tops.append(jnp.concatenate(top_list, axis=0))
    row_totals.append(jnp.concatenate(total_list, axis=0))
    stored = [weight_list]
    attention_rows = jnp.concatenate(pieces_out, axis=1)
    flattened_gradient = output_gradient.reshape(-1, output_gradient.shape[-1])
    adapter_middle = jnp.dot(
        attention_rows, adapter_down_weight, preferred_element_type=jnp.float32
    ).astype(jnp.bfloat16)
    middle_gradient = lax.dot_general(
        flattened_gradient, adapter_up_weight, contract_trailing, preferred_element_type=jnp.float32
    ).astype(jnp.bfloat16)
    weight_piece = lax.all_gather(output_weight_matrix, "dp", axis=1, tiled=True)
    projected = jnp.dot(attention_rows, weight_piece, preferred_element_type=jnp.float32)
    output_running_sum = projected
    back_accum = lax.dot_general(
        flattened_gradient, weight_piece, contract_trailing, preferred_element_type=jnp.float32
    )
    output_running_sum, back_accum = (output_running_sum, back_accum)
    output = (
        output_running_sum
        + jnp.dot(adapter_middle, adapter_up_weight, preferred_element_type=jnp.float32)
    ).astype(jnp.bfloat16)
    output = output.reshape(output_gradient.shape)
    attended_grad = (
        back_accum
        + lax.dot_general(
            middle_gradient,
            adapter_down_weight,
            contract_trailing,
            preferred_element_type=jnp.float32,
        )
    ).astype(jnp.bfloat16)
    token_count = (
        samples * lax.axis_size("dp") * frames * tile_rows * rows_axis * tile_cols * cols_axis
    )
    gradient_norm = token_count ** (-0.5)
    down_part = lax.dot_general(
        attention_rows, middle_gradient, contract_leading, preferred_element_type=jnp.float32
    )
    up_part = lax.dot_general(
        adapter_middle, flattened_gradient, contract_leading, preferred_element_type=jnp.float32
    )
    down_sum, up_sum = lax.psum((down_part, up_part), ("dp", "sh", "sw"))
    key_buffer = jnp.zeros(grid_shape, jnp.bfloat16)
    value_buffer = jnp.zeros(grid_shape, jnp.bfloat16)
    term_shape = (WINDOW, WINDOW, 1, frames, tile_rows, tile_cols, group_span)
    row_deltas = []
    sample = 0
    delta_list = []
    pieces_out = []
    for head_group in range(group_count):
        query_heads = heads_of(query_tokens[sample], head_group)
        key_heads = heads_of(key_window[:, :, sample], head_group)
        value_heads = heads_of(value_window[:, :, sample], head_group)
        grad_heads = heads_of(attended_grad, head_group)
        weights = stored[sample][head_group]
        prob_grad = jnp.einsum(
            "qhd,khd->hqk", grad_heads, value_heads, preferred_element_type=jnp.float32
        )
        row_delta = jnp.sum(weights * prob_grad, axis=-1)
        delta_list.append(row_delta)
        score_grad = (weights * (prob_grad - row_delta[..., None]) * factor).astype(jnp.bfloat16)
        query_part = jnp.einsum(
            "hqk,khd->qhd", score_grad, key_heads, preferred_element_type=jnp.float32
        )
        pieces_out.append(query_part.astype(jnp.bfloat16).reshape(tile_tokens, group_span))
        key_term = jnp.einsum(
            "hqk,qhd->khd", score_grad, query_heads, preferred_element_type=jnp.float32
        )
        value_term = jnp.einsum(
            "hqk,qhd->khd", weights, grad_heads, preferred_element_type=jnp.float32
        )
        place_at = (row_begin, col_begin, sample, 0, 0, 0, head_group * group_span)
        key_buffer = lax.dynamic_update_slice(
            key_buffer, key_term.astype(jnp.bfloat16).reshape(term_shape), place_at
        )
        value_buffer = lax.dynamic_update_slice(
            value_buffer, value_term.astype(jnp.bfloat16).reshape(term_shape), place_at
        )
    row_deltas.append(jnp.concatenate(delta_list, axis=0))
    query_parts = [jnp.concatenate(pieces_out, axis=1).reshape(query_tokens.shape[1:])]
    query_grad = jnp.stack(query_parts, axis=0)
    flat_shape = (rows_axis * cols_axis,) + key_tokens.shape
    key_sum, value_sum = (
        lax.psum_scatter(
            key_buffer.reshape(flat_shape), ("sh", "sw"), scatter_dimension=0, tiled=True
        ).astype(jnp.float32),
        lax.psum_scatter(
            value_buffer.reshape(flat_shape), ("sh", "sw"), scatter_dimension=0, tiled=True
        ).astype(jnp.float32),
    )
    key_grad = key_sum[0].astype(jnp.bfloat16)
    value_grad = value_sum[0].astype(jnp.bfloat16)
    return (
        output,
        query_grad,
        key_grad,
        value_grad,
        down_sum * gradient_norm,
        up_sum * gradient_norm,
    )


def solution(mesh):
    placed = (
        P("dp", None, "sh", "sw", None),
        P("dp", None, "sh", "sw", None),
        P("dp", None, "sh", "sw", None),
        P(),
        P(None, "dp"),
        P(),
        P(),
        P("dp", None, "sh", "sw", None),
    )
    return jax.shard_map(
        body,
        mesh=mesh,
        in_specs=placed,
        out_specs=(
            P("dp", None, "sh", "sw", None),
            P("dp", None, "sh", "sw", None),
            P("dp", None, "sh", "sw", None),
            P("dp", None, "sh", "sw", None),
            P(),
            P(),
        ),
        check_vma=False,
    )
```

profile of v0, /device:TPU:32, one launch (start us, length us, event | category | flops | bytes accessed | tf_op | source)
XLA Modules:
  0.0 858.5 jit_solution(1974098478187125080)
XLA Ops:
  18.9 33.9 %all-gather.6.cloned.1.call-done = bf16[1536,1536]{0,1:T(8,128)(2,1)} async-done(((bf16[1536,96]{0,1:T(8,128)(2,1)}), bf16[1536,1536]{0,1:T(8,128)(2,1)}) %all-gather.6.cloned.1.call-update) | async-done | bytes 4718608 | tf_op jit(solution)/shard_map/all_gather | solution.py:97
  52.8 3.1 fusion.217
  60.6 91.4 %all-gather.10.cloned.1.call-done = bf16[16,2,8,8,1536]{4,3,2,1,0:T(8,128)(2,1)} async-done(((bf16[1,2,8,8,1536]{4,3,2,1,0:T(8,128)(2,1)}), bf16[16,2,8,8,1536]{4,3,2,1,0:T(8,128)(2,1)}) %all-gather.10.cloned.1.call-update) | async-done | bytes 6291472 | tf_op jit(solution)/shard_map/all_gather | solution.py:40
  157.9 92.2 %all-gather.8.cloned.1.call-done = bf16[16,2,8,8,1536]{4,3,2,1,0:T(8,128)(2,1)} async-done(((bf16[1,2,8,8,1536]{4,3,2,1,0:T(8,128)(2,1)}), bf16[16,2,8,8,1536]{4,3,2,1,0:T(8,128)(2,1)}) %all-gather.8.cloned.1.call-update) | async-done | bytes 6291472 | tf_op jit(solution)/shard_map/all_gather | solution.py:41
  262.7 3.0 copy.233
  268.1 3.0 copy.226
  279.0 2.9 copy.212
  327.0 3.0 fusion.54
  330.0 6.0 copy.244
  336.0 3.0 reshape.270
  338.9 3.0 fusion.55
  341.9 6.0 copy.246
  350.7 2.9 fusion.56
  353.6 6.0 copy.248
  362.4 3.0 fusion.57
  365.4 3.0 fusion.58
  368.4 3.3 fusion.59
  372.7 3.4 broadcast.35.clone
  379.2 6.0 copy.250
  388.0 6.0 copy.252
  396.7 6.0 copy.254
  411.4 3.1 copy.257
  418.5 3.0 copy.260
  425.4 2.9 copy.263
  432.3 2.9 copy.266
  439.2 2.9 copy.269
  450.1 3.0 reshape.282
  453.0 3.4 broadcast.35.clone.1
  477.8 4.3 fusion.216
  483.1 141.5 %all-reduce.3.cloned.1.call-done = (f32[1536,64]{0,1:T(8,128)}, f32[64,1536]{1,0:T(8,128)}) async-done(((f32[1536,64]{0,1:T(8,128)}, f32[64,1536]{1,0:T(8,128)}), (f32[1536,64]{0,1:T(8,128)}, f32[64,1536]{1,0:T(8,128)})) %all-reduce.3.cloned.1.call-update) | async-done | bytes 786448 | tf_op jit(solution)/shard_map/psum | solution.py:128
  628.2 109.7 %reduce-scatter.3.cloned.1.call-done = bf16[1,1,2,8,8,1536]{5,4,3,2,1,0:T(8,128)(2,1)} async-done(((bf16[16,1,2,8,8,1536]{5,4,3,2,1,0:T(8,128)(2,1)}), bf16[1,1,2,8,8,1536]{5,4,3,2,1,0:T(8,128)(2,1)}) %reduce-scatter.3.cloned.1.call-update) | async-done | bytes 393232 | tf_op jit(solution)/shard_map/reduce_scatter | solution.py:170
  737.9 113.6 %reduce-scatter.5.cloned.1.call-done = bf16[1,1,2,8,8,1536]{5,4,3,2,1,0:T(8,128)(2,1)} async-done(((bf16[16,1,2,8,8,1536]{5,4,3,2,1,0:T(8,128)(2,1)}), bf16[1,1,2,8,8,1536]{5,4,3,2,1,0:T(8,128)(2,1)}) %reduce-scatter.5.cloned.1.call-update) | async-done | bytes 393232 | tf_op jit(solution)/shard_map/reduce_scatter | solution.py:173
  (229 shorter events, 159.3 us)
Async XLA Ops:
  7.2 11.4 %copy-start = (bf16[1,2,8,8,1536]{4,3,2,1,0:T(8,128)(2,1)S(1)}, bf16[1,2,8,8,1536]{4,3,2,1,0:T(8,128)(2,1)}, u32[]{:S(2)}) copy-start(bf16[1,2,8,8,1536]{4,3,2,1,0:T(8,128)(2,1)} %param.15) | copy-start | bytes 1179652
  7.2 6.2 copy-start.42
  7.2 45.6 %all-gather.6.cloned.1.call-start = ((), (), s32[]{:S(2)}) async-start(), calls=%async_computation.2 | async-start | bytes 5013504 | tf_op jit(solution)/shard_map/all_gather | solution.py:97
  7.9 10.7 %copy-start.26 = (bf16[64,1536]{1,0:T(8,128)(2,1)S(1)}, bf16[64,1536]{1,0:T(8,128)(2,1)}, u32[]{:S(2)}) copy-start(bf16[64,1536]{1,0:T(8,128)(2,1)} %param.14) | copy-start | bytes 589828
  7.9 144.1 %all-gather.10.cloned.1.call-start = ((), (), s32[]{:S(2)}) async-start(), calls=%async_computation.6 | async-start | bytes 6684672 | tf_op jit(solution)/shard_map/all_gather | solution.py:40
  8.7 241.5 %all-gather.8.cloned.1.call-start = ((), (), s32[]{:S(2)}) async-start(), calls=%async_computation.5 | async-start | bytes 6684672 | tf_op jit(solution)/shard_map/all_gather | solution.py:41
  9.4 615.2 %all-reduce.3.cloned.1.call-start = ((), (), s32[]{:S(2)}) async-start(), calls=%async_computation.7 | async-start | bytes 1572864 | tf_op jit(solution)/shard_map/psum | solution.py:128
  18.9 37.1 %copy-start.43 = (bf16[128,64]{0,1:T(8,128)(2,1)}, bf16[128,64]{0,1:T(8,128)(2,1)S(1)}, u32[]{:S(2)}) copy-start(bf16[128,64]{0,1:T(8,128)(2,1)S(1)} %convolution_convert_fusion.19) | copy-start | bytes 49156
  18.9 37.1 %copy-start.25 = (bf16[1536,64]{0,1:T(8,128)(2,1)S(1)}, bf16[1536,64]{0,1:T(8,128)(2,1)}, u32[]{:S(2)}) copy-start(bf16[1536,64]{0,1:T(8,128)(2,1)} %param.13) | copy-start | bytes 589828
  257.5 46.8 %copy-start.6 = (bf16[1152,2,128]{2,1,0:T(2,128)(2,1)}, bf16[1152,2,128]{2,1,0:T(2,128)(2,1)S(1)}, u32[]{:S(2)}) copy-start(bf16[1152,2,128]{2,1,0:T(2,128)(2,1)S(1)} %reshape.250) | copy-start | bytes 1769476
  257.7 41.6 %copy-start.8 = (bf16[1152,2,128]{2,1,0:T(2,128)(2,1)}, bf16[1152,2,128]{2,1,0:T(2,128)(2,1)S(1)}, u32[]{:S(2)}) copy-start(bf16[1152,2,128]{2,1,0:T(2,128)(2,1)S(1)} %reshape.246) | copy-start | bytes 1769476
  257.8 36.4 %copy-start.10 = (bf16[1152,2,128]{2,1,0:T(2,128)(2,1)}, bf16[1152,2,128]{2,1,0:T(2,128)(2,1)S(1)}, u32[]{:S(2)}) copy-start(bf16[1152,2,128]{2,1,0:T(2,128)(2,1)S(1)} %reshape.242) | copy-start | bytes 1769476
  259.9 29.2 %copy-start.12 = (bf16[1152,2,128]{2,1,0:T(2,128)(2,1)}, bf16[1152,2,128]{2,1,0:T(2,128)(2,1)S(1)}, u32[]{:S(2)}) copy-start(bf16[1152,2,128]{2,1,0:T(2,128)(2,1)S(1)} %reshape.237) | copy-start | bytes 1769476
  285.3 2.5 copy-start.40
  314.5 4.4 copy-start.2
  314.6 4.3 copy-start.13
  314.6 4.3 copy-start.35
  316.8 3.4 copy-start.11
  316.8 3.4 copy-start.33
  372.7 365.2 %reduce-scatter.3.cloned.1.call-start = ((), (), s32[]{:S(2)}) async-start(), calls=%async_computation.3 | async-start | bytes 6684672 | tf_op jit(solution)/shard_map/reduce_scatter | solution.py:170
  372.7 3.4 copy-start.14
  405.5 3.0 copy-start.24
  409.5 442.0 %reduce-scatter.5.cloned.1.call-start = ((), (), s32[]{:S(2)}) async-start(), calls=%async_computation.4 | async-start | bytes 6684672 | tf_op jit(solution)/shard_map/reduce_scatter | solution.py:173
  411.4 5.9 copy-start.34
  418.5 5.8 copy-start.32
  453.0 3.4 copy-start.15
  467.5 2.7 copy-start.39
  470.0 2.5 copy-start.38
  472.5 2.5 copy-start.37
  477.7 4.3 copy-start.45
  477.7 4.3 copy-start.27
  477.7 373.7 %copy-start.1 = (bf16[1,2,8,8,1536]{4,3,2,1,0:T(8,128)(2,1)S(1)}, bf16[1,2,8,8,1536]{4,3,2,1,0:T(8,128)(2,1)}, u32[]{:S(2)}) copy-start(bf16[1,2,8,8,1536]{4,3,2,1,0:T(8,128)(2,1)} %param.15) | copy-start | bytes 1179652
  (20 other events, 32.1 us)
Sparse Core Ops, SparseCore 0:
  9.9 42.9 all-gather.5
  55.3 96.7 all-gather.9
  154.5 95.5 all-gather.7
  372.8 251.8 all-reduce.2
  629.3 108.5 reduce-scatter.2
  742.5 108.9 reduce-scatter.4
where the time goes:
time: 869 us; the launch traced here: 859 us
  waiting for transfers between devices  585 us (67%)
  local copies, waits for them, and re-layouts  163 us (19%)
  matrix products  79.5 us (9%)
  between operations  19 us (2%)
  other arithmetic  11.9 us (1%)
    psum x1, waiting for transfers between devices, body(): down_sum, up_sum = lax.psum((down_part, up_part), ('dp', 'sh', 'sw'))  142 us
    reduce_scatter x1, waiting for transfers between devices, body(): lax.psum_scatter(value_buffer.reshape(flat_shape), ('sh', 'sw'), scatter_...  114 us
    reduce_scatter x1, waiting for transfers between devices, body(): lax.psum_scatter(key_buffer.reshape(flat_shape), ('sh', 'sw'), scatter_di...  110 us
    all_gather x1, waiting for transfers between devices, body(): lax.all_gather(value_tokens[None], ('sh', 'sw'), axis=0, tiled=True)  92.2 us
    all_gather x1, waiting for transfers between devices, body(): lax.all_gather(key_tokens[None], ('sh', 'sw'), axis=0, tiled=True)  91.4 us
    reshape x30, local copies, waits for them, and re-layouts, heads_of(): array[..., head_group * group_span:(head_group + 1) * group_span]  41.4 us
    convert_element_type x6, local copies, waits for them, and re-layouts, body(): key_term.astype(jnp.bfloat16).reshape(term_shape)  35.8 us
    all_gather x1, waiting for transfers between devices, body(): lax.all_gather(output_weight_matrix, 'dp', axis=1, tiled=True)  33.9 us
  transfers between devices with their start and end apart: 6, of which 6 were waited for; matrix products, arithmetic and copies ran while one was open for 15% of the time, Pallas kernels for 0%

commit v1 on v0

v1 whole, which is shorter than its diff:
```python
import functools

import jax
import jax.numpy as jnp
from jax import lax
from jax.experimental import pallas as pl
from jax.experimental.pallas import tpu as pltpu
from jax.sharding import PartitionSpec as P

MESH = pl.DeviceIdType.MESH
HEADS = 12
HEAD = 128
WINDOW = 3
GROUP = 3
GRID = 4
TOK = 128
RANK = 64
FEAT = 1536
SPAN = GROUP * HEAD
SHARD = 96
TOKENS = 32768
BF = jnp.bfloat16
F32 = jnp.float32
NT = (((1,), (1,)), ((), ()))
TN = (((0,), (0,)), ((), ()))
NN = (((1,), (0,)), ((), ()))


def dot(a, b, dims):
    return lax.dot_general(a, b, dims, preferred_element_type=F32)


class Sems:
    def __init__(self, send, recv):
        self.send, self.recv, self.used = send, recv, 0

    def copy(self, src, dst, device):
        slot = self.used
        self.used += 1
        made = pltpu.make_async_remote_copy(
            src_ref=src,
            dst_ref=dst,
            send_sem=self.send.at[slot],
            recv_sem=self.recv.at[slot],
            device_id=device,
            device_id_type=MESH,
        )
        made.start()
        return made


def place():
    return lax.axis_index("dp"), lax.axis_index("sh"), lax.axis_index("sw")


def turn(index, by, size):
    return lax.rem(index + by, size)


def flip(dp, bit):
    return dp + bit - 2 * bit * lax.rem(lax.div(dp, bit), 2)


def greet(devices):
    barrier = pltpu.get_barrier_semaphore()
    for device in devices:
        pl.semaphore_signal(barrier, inc=1, device_id=device, device_id_type=MESH)
    pl.semaphore_wait(barrier, len(devices))


SPREAD_COPIES = 9 + 24 + 15 + 3


def spread_kernel(
    q_ref, k_ref, v_ref, og_ref, w_ref, down_ref, up_ref,
    qz, kall, vall, doz, wt, midg,
    qs, ks, vs, dos, send, recv,
):
    dp, sh, sw = place()
    sems = Sems(send, recv)
    row_peer = [(dp, turn(sh, d, GRID), sw) for d in (1, 2, 3)]
    col_peer = [(dp, sh, turn(sw, d, GRID)) for d in (1, 2, 3)]
    x_peer = [(turn(dp, 4 * d, 16), sh, sw) for d in (1, 2, 3)]
    zlo = (flip(dp, 2), sh, sw)
    twin = (flip(dp, 1), sh, sw)
    for h in range(HEADS):
        cols = slice(h * HEAD, (h + 1) * HEAD)
        ks[h] = k_ref[:, cols]
        vs[h] = v_ref[:, cols]
        qs[h] = q_ref[:, cols]
    for j in range(GROUP):
        kall[j, sw, sh] = ks[sh * GROUP + j]
        vall[j, sw, sh] = vs[sh * GROUP + j]
        qz[j, sh] = qs[sh * GROUP + j]
    own_rows = pl.ds(pl.multiple_of(dp * SHARD, SHARD), SHARD)
    wt[own_rows, :] = w_ref[...]
    greet(row_peer + col_peer + x_peer + [zlo, twin])

    pending = []

    def rows_to(stack, peer):
        return stack.at[pl.ds(peer[1] * GROUP, GROUP)]

    k_in, v_in, q_in = [], [], []
    for peer in row_peer:
        k_in.append(sems.copy(rows_to(ks, peer), kall.at[:, sw, sh], peer))
        v_in.append(sems.copy(rows_to(vs, peer), vall.at[:, sw, sh], peer))

    def shard_of(owner):
        return wt.at[pl.ds(pl.multiple_of(owner * SHARD, SHARD), SHARD)]

    def pass_on(owner, peer):
        return sems.copy(shard_of(owner), shard_of(owner), peer)

    zlo_in = pass_on(dp, zlo)
    own_in = [pass_on(dp, peer) for peer in x_peer]
    twin_in = [pass_on(dp, twin)]

    def down_the_row(row):
        for stack in (kall, vall):
            for peer in col_peer:
                block = stack.at[:, sw, row]
                pending.append(sems.copy(block, block, peer))

    down_the_row(sh)
    for peer in row_peer:
        q_in.append(sems.copy(rows_to(qs, peer), qz.at[:, sh], peer))

    mid = dot(og_ref[...], up_ref[...], NT).astype(BF)
    midg[...] = mid

    zlo_in.wait_recv()
    other_in = [pass_on(flip(dp, 2), peer) for peer in x_peer]
    twin_in.append(pass_on(flip(dp, 2), twin))
    for d in (0, 2, 1):
        k_in[d].wait_recv()
        v_in[d].wait_recv()
        down_the_row(turn(sh, GRID - d - 1, GRID))
    for d in (0, 2, 1):
        owner = turn(dp, 16 - 4 * (d + 1), 16)
        own_in[d].wait_recv()
        twin_in.append(pass_on(owner, twin))
        other_in[d].wait_recv()
        twin_in.append(pass_on(flip(owner, 2), twin))
    for made in twin_in:
        made.wait_recv()

    do_in = []
    for d in (1, 3, 2, 0):
        target = turn(sh, d, GRID)
        cols = pl.ds(pl.multiple_of(target * SPAN, HEAD), SPAN)
        part = dot(og_ref[...], wt[:, cols], NN) + dot(midg[...], down_ref[:, cols], NN)
        part = part.astype(BF)
        for j in range(GROUP):
            piece = part[:, j * HEAD : (j + 1) * HEAD]
            if d:
                dos[target * GROUP + j] = piece
            else:
                doz[j, sh] = piece
        if d:
            peer = (dp, target, sw)
            do_in.append(sems.copy(rows_to(dos, peer), doz.at[:, sh], peer))
    for made in k_in + v_in + own_in + other_in + twin_in + [zlo_in]:
        made.wait_send()
    for made in q_in + do_in + pending:
        made.wait()


def attend_kernel(table, qz, doz, kall, vall, o_out, dq_out, dk_out, dv_out, dk, dv):
    factor = HEAD ** (-0.5)
    dk[...] = jnp.zeros_like(dk)
    dv[...] = jnp.zeros_like(dv)

    def unit(step, carry):
        j = step // GRID
        i = step % GRID
        row = table[0, i]
        col = table[1, i]
        q = qz[j, i]
        do = doz[j, i]

        def window(stack, c):
            return stack[j, col + c, pl.ds(row, WINDOW)].reshape(WINDOW * TOK, HEAD)

        scores = [dot(window(kall, c), q, NT) * factor for c in range(WINDOW)]
        top = functools.reduce(jnp.maximum, [jnp.max(s, axis=0, keepdims=True) for s in scores])
        expo = [jnp.exp(s - top) for s in scores]
        total = sum(jnp.sum(e, axis=0, keepdims=True) for e in expo)
        inverse = 1.0 / total
        prob = [(e * inverse).astype(BF) for e in expo]
        att = sum(dot(window(vall, c), prob[c], TN) for c in range(WINDOW))
        delta = jnp.sum(att * do.astype(F32).T, axis=0, keepdims=True)
        o_out[i, j] = att.T.astype(BF)
        dq = jnp.zeros((HEAD, TOK), F32)
        for c in range(WINDOW):
            dprob = dot(window(vall, c), do, NT)
            dscore = (prob[c].astype(F32) * (dprob - delta) * factor).astype(BF)
            dq = dq + dot(window(kall, c), dscore, TN)
            spot = (j, col + c, pl.ds(row, WINDOW))
            dk[spot] += dot(dscore, q, NN).reshape(WINDOW, TOK, HEAD)
            dv[spot] += dot(prob[c], do, NN).reshape(WINDOW, TOK, HEAD)
        dq_out[i, j] = dq.T.astype(BF)
        return carry

    lax.fori_loop(0, GROUP * GRID, unit, 0)
    for j in range(GROUP):
        for c in range(GRID):
            for r in range(GRID):
                dk_out[c, r, j] = dk[j, c, r].astype(BF)
                dv_out[c, r, j] = dv[j, c, r].astype(BF)


RETURN_COPIES = 6 + 6 + 6 + 3 + 3 + 15 + 3 + 3


def return_kernel(
    o_ref, dq_ref, dk_ref, dv_ref, wt_ref, up_ref, downt_ref, og_ref, midg_ref,
    out, dq_out, dk_out, dv_out, grads,
    oh, dqh, dkh, dvh, rk, rv, ksum, vsum, att, ad, ry, zsrc, rz, dpsrc, rdp, full, send, recv,
):
    dp, sh, sw = place()
    sems = Sems(send, recv)
    row_peer = [(dp, turn(sh, d, GRID), sw) for d in (1, 2, 3)]
    col_peer = [(dp, sh, turn(sw, d, GRID)) for d in (1, 2, 3)]
    dp_peer = [(turn(dp, d, 16), sh, sw) for d in range(1, 16)]
    greet(row_peer + col_peer + dp_peer)

    k_in = [sems.copy(dk_ref.at[p[2]], rk.at[n], p) for n, p in enumerate(col_peer)]
    v_in = [sems.copy(dv_ref.at[p[2]], rv.at[n], p) for n, p in enumerate(col_peer)]
    home = pl.ds(sh * GROUP, GROUP)
    o_in = [sems.copy(o_ref.at[p[1]], oh.at[home], p) for p in row_peer]
    q_in = [sems.copy(dq_ref.at[p[1]], dqh.at[home], p) for p in row_peer]
    for j in range(GROUP):
        oh[sh * GROUP + j] = o_ref[sh, j]
        dqh[sh * GROUP + j] = dq_ref[sh, j]

    for made in o_in:
        made.wait_recv()
    for h in range(HEADS):
        att[:, h * HEAD : (h + 1) * HEAD] = oh[h]
    lora = dot(att[...], downt_ref[...], NT).astype(BF)
    ad[pl.ds(0, RANK), :] = dot(midg_ref[...], att[...], TN).astype(BF)
    ad[pl.ds(RANK, RANK), :] = dot(lora, og_ref[...], TN).astype(BF)

    part = 2 * RANK // GRID

    def strip(owner):
        return pl.ds(pl.multiple_of(owner * part, part), part)

    y_in = [sems.copy(ad.at[strip(p[2])], ry.at[n], p) for n, p in enumerate(col_peer)]
    for n in range(GRID):
        block = slice(n * SPAN, (n + 1) * SPAN)
        out[:, block] = (
            dot(att[...], wt_ref[block, :], NT) + dot(lora, up_ref[:, block], NN)
        ).astype(BF)

    for made in y_in:
        made.wait_recv()
    summed = ad[strip(sw), :].astype(F32)
    for n in range(3):
        summed = summed + ry[n].astype(F32)
    for n in range(GRID):
        zsrc[n] = summed[:, n * SPAN : (n + 1) * SPAN].astype(BF)
    z_in = [sems.copy(zsrc.at[p[1]], rz.at[n], p) for n, p in enumerate(row_peer)]

    back_in = []
    for made_in, own, got, total, there in (
        (k_in, dk_ref, rk, ksum, dkh),
        (v_in, dv_ref, rv, vsum, dvh),
    ):
        for made in made_in:
            made.wait_recv()
        for r in range(GRID):
            for j in range(GROUP):
                piece = own[sw, r, j].astype(F32)
                for n in range(3):
                    piece = piece + got[n, r, j].astype(F32)
                total[r, j] = piece.astype(BF)
        for p in row_peer:
            back_in.append(sems.copy(total.at[p[1]], there.at[home], p))
        for j in range(GROUP):
            there[sh * GROUP + j] = total[sh, j]

    for made in z_in:
        made.wait_recv()
    summed = zsrc[sh].astype(F32)
    for n in range(3):
        summed = summed + rz[n].astype(F32)
    dpsrc[...] = summed.astype(BF)
    rdp[dp] = dpsrc[...]
    d_in = [sems.copy(dpsrc, rdp.at[dp], p) for p in dp_peer]

    for made in q_in:
        made.wait_recv()
    for h in range(HEADS):
        dq_out[:, h * HEAD : (h + 1) * HEAD] = dqh[h]

    for made in d_in:
        made.wait_recv()
    summed = rdp[0].astype(F32)
    for n in range(1, 16):
        summed = summed + rdp[n].astype(F32)
    full[sw, sh] = summed.astype(BF)
    spot = full.at[sw, sh]
    g_in = [sems.copy(spot, spot, p) for p in row_peer]
    for made in g_in:
        made.wait_recv()
    spot = full.at[sw]
    h_in = [sems.copy(spot, spot, p) for p in col_peer]

    for made in back_in:
        made.wait_recv()
    for h in range(HEADS):
        dk_out[:, h * HEAD : (h + 1) * HEAD] = dkh[h]
        dv_out[:, h * HEAD : (h + 1) * HEAD] = dvh[h]
    for made in h_in:
        made.wait_recv()
    norm = TOKENS ** (-0.5)
    for c in range(GRID):
        for r in range(GRID):
            grads[c * part : (c + 1) * part, r * SPAN : (r + 1) * SPAN] = (
                full[c, r].astype(F32) * norm
            )
    for made in k_in + v_in + o_in + q_in + y_in + z_in + back_in + d_in + g_in + h_in:
        made.wait_send()


VM = pl.BlockSpec(memory_space=pltpu.VMEM)
SM = pl.BlockSpec(memory_space=pltpu.SMEM)
LIMIT = 48 << 20


def shaped(*dims, kind=BF):
    return jax.ShapeDtypeStruct(dims, kind)


def body(query, key, value, first_tile, weight, down, up, out_grad):
    shape = query.shape
    q, k, v, og = (a.reshape(TOK, FEAT) for a in (query, key, value, out_grad))
    wt_shard = weight.T
    downt = down.T
    stack = (GROUP, GRID, TOK, HEAD)
    grid = (GROUP, GRID, GRID, TOK, HEAD)
    heads = (HEADS, TOK, HEAD)
    dma = pltpu.SemaphoreType.DMA
    qz, kall, vall, doz, wt, midg = pl.pallas_call(
        spread_kernel,
        name="spread",
        out_shape=(
            shaped(*stack), shaped(*grid), shaped(*grid), shaped(*stack),
            shaped(FEAT, FEAT), shaped(TOK, RANK),
        ),
        in_specs=[VM] * 7,
        out_specs=[VM] * 6,
        scratch_shapes=[pltpu.VMEM(heads, BF)] * 4 + [dma((SPREAD_COPIES,)), dma((SPREAD_COPIES,))],
        compiler_params=pltpu.CompilerParams(
            collective_id=0, has_side_effects=True, vmem_limit_bytes=LIMIT
        ),
    )(q, k, v, og, wt_shard, downt, up)

    table = lax.dynamic_index_in_dim(first_tile, lax.axis_index("sw"), axis=2, keepdims=False)
    by_row = (GRID, GROUP, TOK, HEAD)
    by_spot = (GRID, GRID, GROUP, TOK, HEAD)
    o, dq, dk, dv = pl.pallas_call(
        attend_kernel,
        name="attend",
        out_shape=(shaped(*by_row), shaped(*by_row), shaped(*by_spot), shaped(*by_spot)),
        in_specs=[SM] + [VM] * 4,
        out_specs=[VM] * 4,
        scratch_shapes=[pltpu.VMEM(grid, F32)] * 2,
        compiler_params=pltpu.CompilerParams(vmem_limit_bytes=LIMIT),
    )(table, qz, doz, kall, vall)

    flat = (TOK, FEAT)
    part = 2 * RANK // GRID
    output, dq, dk, dv, grads = pl.pallas_call(
        return_kernel,
        name="bring_home",
        out_shape=(
            shaped(*flat), shaped(*flat), shaped(*flat), shaped(*flat),
            shaped(2 * RANK, FEAT, kind=F32),
        ),
        in_specs=[VM] * 9,
        out_specs=[VM] * 5,
        scratch_shapes=[
            pltpu.VMEM(heads, BF), pltpu.VMEM(heads, BF), pltpu.VMEM(heads, BF), pltpu.VMEM(heads, BF),
            pltpu.VMEM((3,) + by_row, BF), pltpu.VMEM((3,) + by_row, BF),
            pltpu.VMEM(by_row, BF), pltpu.VMEM(by_row, BF),
            pltpu.VMEM(flat, BF),
            pltpu.VMEM((2 * RANK, FEAT), BF),
            pltpu.VMEM((3, part, FEAT), BF),
            pltpu.VMEM((GRID, part, SPAN), BF),
            pltpu.VMEM((3, part, SPAN), BF),
            pltpu.VMEM((part, SPAN), BF),
            pltpu.VMEM((16, part, SPAN), BF),
            pltpu.VMEM((GRID, GRID, part, SPAN), BF),
            dma((RETURN_COPIES,)), dma((RETURN_COPIES,)),
        ],
        compiler_params=pltpu.CompilerParams(
            collective_id=1, has_side_effects=True, vmem_limit_bytes=LIMIT
        ),
    )(o, dq, dk, dv, wt, up, downt, og, midg)
    return (
        output.reshape(shape),
        dq.reshape(shape),
        dk.reshape(shape),
        dv.reshape(shape),
        grads[:RANK].T,
        grads[RANK:],
    )


def solution(mesh):
    tiles = P("dp", None, "sh", "sw", None)
    return jax.shard_map(
        body,
        mesh=mesh,
        in_specs=(tiles, tiles, tiles, P(), P(None, "dp"), P(), P(), tiles),
        out_specs=(tiles, tiles, tiles, tiles, P(), P()),
        check_vma=False,
    )
```

time: 869 us -> 186 us (0.21); the launches traced: 859 us -> 186 us
  waiting for transfers between devices: 585 us -> 0 us
  Pallas kernels: 0 us -> 170 us
  local copies, waits for them, and re-layouts: 163 us -> 15.1 us
  matrix products: 79.5 us -> 0 us
  between operations: 19 us -> 0.71 us
  other arithmetic: 11.9 us -> 0 us
    reduce_scatter x2 -> x0, waiting for transfers between devices: 223 us -> none  [the longest x1 114 us: body(): lax.psum_scatter(value_buffer.reshape(flat_shape), ('sh', 'sw'), scatter_...]
    all_gather x3 -> x0, waiting for transfers between devices: 218 us -> none  [the longest x1 92.2 us: body(): lax.all_gather(value_tokens[None], ('sh', 'sw'), axis=0, tiled=True)]
    pallas_call x0 -> x3, Pallas kernels: none -> 170 us  [the longest x1 85.8 us: body(): pl.pallas_call(return_kernel, name='bring_home', out_shape=(shaped(*flat)...]
    psum x1 -> x0, waiting for transfers between devices: 142 us -> none  [body(): down_sum, up_sum = lax.psum((down_part, up_part), ('dp', 'sh', 'sw'))]
    reshape x42 -> x0, local copies, waits for them, and re-layouts: 75.1 us -> none  [the longest x30 41.4 us: heads_of(): array[..., head_group * group_span:(head_group + 1) * group_span]]
    dot_general x38 -> x0, matrix products: 63.8 us -> none  [the longest x6 18.2 us: body(): jnp.einsum('hqk,qhd->khd', score_grad, query_heads, preferred_element_typ...]
    convert_element_type x18 -> x0, local copies, waits for them, and re-layouts: 54.4 us -> none  [the longest x6 35.8 us: body(): key_term.astype(jnp.bfloat16).reshape(term_shape)]
    sub x6 -> x0, matrix products: 15.7 us -> none  [body(): exponent = jnp.exp(scores - row_top[..., None])]
  transfers between devices with their start and end apart: 6 -> 0, of which waited for: 6 -> 0; matrix products, arithmetic and copies ran while one was open for 15% -> 0% of each run, Pallas kernels for 0% -> 0%
where the time goes in v1:
time: 186 us
  Pallas kernels  170 us (91%)
  local copies, waits for them, and re-layouts  15.1 us (8%)
    pallas_call x1, Pallas kernels, body(): pl.pallas_call(return_kernel, name='bring_home', out_shape=(shaped(*flat)...  85.8 us
    pallas_call x1, Pallas kernels, body(): pl.pallas_call(spread_kernel, name='spread', out_shape=(shaped(*stack), s...  64.7 us
    pallas_call x1, Pallas kernels, body(): pl.pallas_call(attend_kernel, name='attend', out_shape=(shaped(*by_row),...  19.8 us
    unnamed x32, local copies, waits for them, and re-layouts  14 us

profile of v1, /device:TPU:32, one launch (start us, length us, event | category | flops | bytes accessed | tf_op | source)
XLA Modules:
  0.0 186.1 jit_solution(15333751146274333727)
XLA Ops:
  0.6 0.0 copy-start
  0.7 0.7 copy-done
  1.3 0.2 dynamic-slice_reduce_fusion.table
  1.5 0.0 copy-start.1
  1.5 1.0 copy-done.1
  2.5 0.9 copy-done.6
  3.5 0.0 copy-start.8
  3.5 0.9 copy-done.8
  4.4 0.0 copy-start.10
  4.4 1.0 copy-done.10
  5.4 0.0 copy-start.11
  5.4 1.0 copy-done.11
  6.4 0.0 copy-start.12
  6.4 1.0 copy-done.12
  7.4 0.0 copy-start.13
  7.4 1.0 copy-done.13
  8.3 64.7 %spread.1 = (bf16[3,4,128,128]{3,2,1,0:T(8,128)(2,1)S(1)}, bf16[3,4,4,128,128]{4,3,2,1,0:T(8,128)(2,1)S(1)}, bf16[3,4,4,128,128]{4,3,2,1,0:T(8,128)(2,1)S(1)}, b...) custom-call(bf16[128,1536]{1,0:T(8,128)(2,1)S(1)} %bitcast.20, ...), custom_call_target="tpu_custom_call" | custom-call | tf_op jit(solution)/shard_map/spread/pallas_call | solution.py:346
  73.0 0.0 copy-start.4
  73.0 1.2 copy-done.4
  74.2 1.1 copy-done.5
  75.4 19.8 %attend.1 = (bf16[4,3,128,128]{3,2,1,0:T(8,128)(2,1)S(1)}, bf16[4,3,128,128]{3,2,1,0:T(8,128)(2,1)S(1)}, bf16[4,4,3,128,128]{4,3,2,1,0:T(8,128)(2,1)S(1)}, bf16[4,4,3,128,128]{4,3,2,1,0:T(8,128)(2,1)S(1)}) custom-call(s32[2,4]{1,0:T(2,128)S(1)} %dynamic-slice_reduce_fusion.table, bf16[3,4,128,128]{3,2,1,0:T(8,128)(2,1)S(1)} %get-tuple-element.21.qz, ...), custom_call_target="tpu_custom_call" | custom-call | tf_op jit(solution)/shard_map/attend/pallas_call | solution.py:364
  95.2 0.0 copy-start.3
  95.2 1.2 copy-done.3
  96.4 0.0 copy-done.2
  96.4 0.0 copy-done.7
  96.4 0.0 copy-done.9
  96.4 85.8 %bring_home.1 = (bf16[128,1536]{1,0:T(8,128)(2,1)S(1)}, bf16[128,1536]{1,0:T(8,128)(2,1)S(1)}, bf16[128,1536]{1,0:T(8,128)(2,1)S(1)}, bf16[128,1536]{1,0:T(8,128)(2,1)S(1)}, f32[128,1536]{1,0:T(8,128)S(1)}) custom-call(bf16[4,3,128,128]{3,2,1,0:T(8,128)(2,1)S(1)} %get-tuple-element.25.o_ref, bf16[4,3,128,128]{3,2,1,0:T(8,128)(2,1)S(1)} %get-tuple-element.26.dq_ref, ...), custom_call_target="tpu_custom_call" | custom-call | tf_op jit(solution)/shard_map/bring_home/pallas_call | solution.py:376
  182.2 0.9 fusion
  183.1 0.7 copy.18
  183.9 0.7 copy.19
  184.6 0.7 copy.20
  185.3 0.7 copy.21
  (5 shorter events, 0.0 us)
Async XLA Ops:
  0.6 0.7 copy-start
  1.5 1.0 copy-start.1
  2.5 0.9 copy-start.6
  3.5 0.9 copy-start.8
  4.4 1.0 copy-start.10
  5.4 1.0 copy-start.11
  6.4 1.0 copy-start.12
  7.4 1.0 copy-start.13
  73.0 1.2 copy-start.4
  74.2 1.1 copy-start.5
  75.4 21.0 %copy-start.2 = (bf16[1,2,8,8,1536]{4,3,2,1,0:T(8,128)(2,1)S(1)}, bf16[1,2,8,8,1536]{4,3,2,1,0:T(8,128)(2,1)}, u32[]{:S(2)}) copy-start(bf16[1,2,8,8,1536]{4,3,2,1,0:T(8,128)(2,1)} %param.15) | copy-start | bytes 1179652
  75.4 21.0 %copy-start.7 = (bf16[1536,64]{0,1:T(8,128)(2,1)S(1)}, bf16[1536,64]{0,1:T(8,128)(2,1)}, u32[]{:S(2)}) copy-start(bf16[1536,64]{0,1:T(8,128)(2,1)} %param.13) | copy-start | bytes 589828
  75.4 21.0 %copy-start.9 = (bf16[64,1536]{1,0:T(8,128)(2,1)S(1)}, bf16[64,1536]{1,0:T(8,128)(2,1)}, u32[]{:S(2)}) copy-start(bf16[64,1536]{1,0:T(8,128)(2,1)} %up_ref.3) | copy-start | bytes 589828
  95.2 1.2 copy-start.3

commit v2 on v1

v2 whole, which is shorter than its diff:
```python
import functools

import jax
import jax.numpy as jnp
from jax import lax
from jax.experimental import pallas as pl
from jax.experimental.pallas import tpu as pltpu
from jax.sharding import PartitionSpec as P

MESH = pl.DeviceIdType.MESH
HEADS = 12
HEAD = 128
WINDOW = 3
GROUP = 3
GRID = 4
TOK = 128
RANK = 64
FEAT = 1536
SPAN = GROUP * HEAD
SHARD = 96
TOKENS = 32768
BF = jnp.bfloat16
F32 = jnp.float32
NT = (((1,), (1,)), ((), ()))
TN = (((0,), (0,)), ((), ()))
NN = (((1,), (0,)), ((), ()))


def dot(a, b, dims):
    return lax.dot_general(a, b, dims, preferred_element_type=F32)


class Sems:
    def __init__(self, send, recv):
        self.send, self.recv, self.used = send, recv, 0

    def copy(self, src, dst, device):
        slot = self.used
        self.used += 1
        made = pltpu.make_async_remote_copy(
            src_ref=src,
            dst_ref=dst,
            send_sem=self.send.at[slot],
            recv_sem=self.recv.at[slot],
            device_id=device,
            device_id_type=MESH,
        )
        made.start()
        return made


def place():
    return lax.axis_index("dp"), lax.axis_index("sh"), lax.axis_index("sw")


def turn(index, by, size):
    return lax.rem(index + by, size)


def flip(dp, bit):
    return dp + bit - 2 * bit * lax.rem(lax.div(dp, bit), 2)


COPIES = 15 + 36 + 18 + 18 + 36 + 27


def kernel(
    table, q_hbm, k_hbm, v_hbm, og_hbm, w_hbm, down_hbm, up_hbm,
    out, dq_out, dk_out, dv_out, grads,
    q_in, k_in, v_in, og, w_in, downt, up,
    qs, ks, vs, dos, wt, mid,
    kj, vj, qj, doj, prob, att, dsl, oj, dqj, dkp, dvp,
    relk, relv, cmbk, cmbv, nearkv, farkv, sumk, sumv,
    oh, dqh, dkh, dvh, rows, ad, ry, zsrc, rz, dpsrc, rdp, full,
    local, send, recv,
):
    dp, sh, sw = place()
    sems = Sems(send, recv)
    factor = HEAD ** (-0.5)
    row_peer = [(dp, turn(sh, d, GRID), sw) for d in (1, 2, 3)]
    col_peer = [(dp, sh, turn(sw, d, GRID)) for d in (1, 2, 3)]
    dp_peer = [(turn(dp, d, 16), sh, sw) for d in range(1, 16)]
    after, before = col_peer[0], col_peer[2]
    east, west = dp_peer[3], dp_peer[11]
    mate = flip(dp, 2)
    zlo = (mate, sh, sw)
    twin = (flip(dp, 1), sh, sw)
    peers = row_peer + col_peer + dp_peer

    loads = []
    for n, (src, dst) in enumerate(
        ((w_hbm, w_in), (k_hbm, k_in), (v_hbm, v_in), (og_hbm, og), (up_hbm, up), (q_hbm, q_in), (down_hbm, downt))
    ):
        made = pltpu.make_async_copy(src, dst, local.at[n])
        made.start()
        loads.append(made)
    barrier = pltpu.get_barrier_semaphore()
    for device in peers:
        pl.semaphore_signal(barrier, inc=1, device_id=device, device_id_type=MESH)

    def shard_of(owner):
        return wt.at[pl.ds(pl.multiple_of(owner * SHARD, SHARD), SHARD)]

    def pass_on(owner, peer):
        return sems.copy(shard_of(owner), shard_of(owner), peer)

    loads[0].wait()
    wt[pl.ds(pl.multiple_of(dp * SHARD, SHARD), SHARD), :] = w_in[...]
    loads[1].wait()
    loads[2].wait()
    for h in range(HEADS):
        cols = slice(h * HEAD, (h + 1) * HEAD)
        ks[h] = k_in[:, cols]
        vs[h] = v_in[:, cols]
    pl.semaphore_wait(barrier, len(peers))

    done = []

    def scatter(stack, dst, j):
        made = [sems.copy(stack.at[p[1] * GROUP + j], dst, p) for p in row_peer]
        done.extend(made)
        return made

    def take(copies):
        for made in copies:
            made.wait_recv()

    def send_kv(j):
        return scatter(ks, kj[j].at[sw, sh], j) + scatter(vs, vj[j].at[sw, sh], j)

    kv = [send_kv(0)]
    mate_in = pass_on(dp, zlo)
    own_east, own_west = pass_on(dp, east), pass_on(dp, west)
    twin_in = [pass_on(dp, twin)]
    for j in range(GROUP):
        kj[j][sw, sh] = ks[sh * GROUP + j]
        vj[j][sw, sh] = vs[sh * GROUP + j]
    loads[3].wait()
    loads[4].wait()
    mid[...] = dot(og[...], up[...], NT).astype(BF)
    loads[5].wait()
    for h in range(HEADS):
        qs[h] = q_in[:, h * HEAD : (h + 1) * HEAD]
    for j in range(GROUP):
        qj[j][sh] = qs[sh * GROUP + j]
    loads[6].wait()

    mate_in.wait_recv()
    mate_east, mate_west = pass_on(mate, east), pass_on(mate, west)
    twin_in.append(pass_on(mate, twin))

    near, relay = [], []

    def spread_near(j):
        take(kv[j])
        near.append(
            (
                sems.copy(kj[j].at[sw], kj[j].at[sw], after),
                sems.copy(vj[j].at[sw], vj[j].at[sw], before),
                sems.copy(kj[j].at[sw], kj[j].at[sw], before),
                sems.copy(vj[j].at[sw], vj[j].at[sw], after),
            )
        )
        done.extend(near[j])

    def spread_far(j):
        take(near[j][:2])
        left, right = turn(sw, 3, GRID), turn(sw, 1, GRID)
        relay.append(
            (
                sems.copy(kj[j].at[left], kj[j].at[left], after),
                sems.copy(vj[j].at[right], vj[j].at[right], before),
            )
        )
        done.extend(relay[j])

    spread_near(0)
    kv.append(send_kv(1))
    q_got = [scatter(qs, qj[0].at[sh], 0)]

    def owner_at(step):
        return turn(dp, step, 16)

    own_east.wait_recv()
    own_far = pass_on(owner_at(12), east)
    twin_in.append(pass_on(owner_at(12), twin))
    own_west.wait_recv()
    twin_in.append(pass_on(owner_at(4), twin))

    spread_far(0)
    mate_west.wait_recv()
    mate_far = pass_on(flip(owner_at(4), 2), west)
    twin_in.append(pass_on(flip(owner_at(4), 2), twin))
    mate_east.wait_recv()
    twin_in.append(pass_on(flip(owner_at(12), 2), twin))

    spread_near(1)
    kv.append(send_kv(2))
    spread_far(1)
    own_far.wait_recv()
    twin_in.append(pass_on(owner_at(8), twin))
    mate_far.wait_recv()
    twin_in.append(pass_on(flip(owner_at(8), 2), twin))
    done.extend(twin_in + [mate_in, own_east, own_west, mate_east, mate_west, own_far, mate_far])
    spread_near(2)
    q_got.append(scatter(qs, qj[1].at[sh], 1))
    q_got.append(scatter(qs, qj[2].at[sh], 2))

    def window(stack, i, c):
        row, col = table[0, i, sw], table[1, i, sw]
        return stack[col + c, pl.ds(row, WINDOW)].reshape(WINDOW * TOK, HEAD)

    o_got = []

    def forward(j):
        take(near[j][2:])
        take(relay[j])
        take(q_got[j])

        def unit(i, carry):
            q = qj[j][i]
            scores = [dot(window(kj[j], i, c), q, NT) * factor for c in range(WINDOW)]
            top = functools.reduce(
                jnp.maximum, [jnp.max(s, axis=0, keepdims=True) for s in scores]
            )
            expo = [jnp.exp(s - top) for s in scores]
            total = sum(jnp.sum(e, axis=0, keepdims=True) for e in expo)
            inverse = 1.0 / total
            attended = jnp.zeros((HEAD, TOK), F32)
            for c in range(WINDOW):
                p = (expo[c] * inverse).astype(BF)
                prob[j, i, c] = p.reshape(WINDOW, TOK, TOK)
                attended = attended + dot(window(vj[j], i, c), p, TN)
            att[j, i] = attended
            oj[j][i] = attended.T.astype(BF)
            return carry

        lax.fori_loop(0, GRID, unit, 0)
        oh[sh * GROUP + j] = oj[j][sh]
        made = [sems.copy(oj[j].at[p[1]], oh.at[sh * GROUP + j], p) for p in row_peer]
        done.extend(made)
        o_got.extend(made)

    def project_back():
        take(twin_in)
        made = [[], [], []]
        for d in (1, 3, 2, 0):
            target = turn(sh, d, GRID)
            cols = pl.ds(pl.multiple_of(target * SPAN, HEAD), SPAN)
            part = dot(og[...], wt[:, cols], NN) + dot(mid[...], downt[:, cols], NN)
            part = part.astype(BF)
            for j in range(GROUP):
                piece = part[:, j * HEAD : (j + 1) * HEAD]
                if d:
                    dos[target * GROUP + j] = piece
                else:
                    doj[j][sh] = piece
        for j in range(GROUP):
            made[j] = scatter(dos, doj[j].at[sh], j)
        return made

    do_got = project_back()
    spread_far(2)
    forward(0)
    forward(1)
    forward(2)

    dq_got, rs_first, rs_second, back_got = [], [], [], []

    def backward(j):
        take(do_got[j])

        def unit(i, carry):
            do = doj[j][i]
            delta = jnp.sum(att[j, i] * do.astype(F32).T, axis=0, keepdims=True)
            dq = jnp.zeros((HEAD, TOK), F32)
            for c in range(WINDOW):
                dprob = dot(window(vj[j], i, c), do, NT)
                p = prob[j, i, c].reshape(WINDOW * TOK, TOK).astype(F32)
                dscore = (p * (dprob - delta) * factor).astype(BF)
                dsl[i, c] = dscore.reshape(WINDOW, TOK, TOK)
                dq = dq + dot(window(kj[j], i, c), dscore, TN)
            dqj[j][i] = dq.T.astype(BF)
            return carry

        lax.fori_loop(0, GRID, unit, 0)
        dqh[sh * GROUP + j] = dqj[j][sh]
        made = [sems.copy(dqj[j].at[p[1]], dqh.at[sh * GROUP + j], p) for p in row_peer]
        done.extend(made)
        dq_got.extend(made)
        q_all = qj[j][...].reshape(GRID * TOK, HEAD)
        do_all = doj[j][...].reshape(GRID * TOK, HEAD)

        def column(c, carry):
            def gathered(load):
                lines = []
                for r in range(GRID):
                    blocks = []
                    for i in range(GRID):
                        rr = r - table[0, i, sw]
                        cc = c - table[1, i, sw]
                        inside = (rr >= 0) & (rr < WINDOW) & (cc >= 0) & (cc < WINDOW)
                        block = load(i, jnp.clip(cc, 0, WINDOW - 1), jnp.clip(rr, 0, WINDOW - 1))
                        blocks.append(jnp.where(inside, block, jnp.zeros_like(block)))
                    lines.append(jnp.concatenate(blocks, axis=1))
                return jnp.concatenate(lines, axis=0)

            shape = (GRID, TOK, HEAD)
            dkp[j][c] = dot(gathered(lambda i, a, b: dsl[i, a, b]), q_all, NN).astype(BF).reshape(shape)
            dvp[j][c] = dot(gathered(lambda i, a, b: prob[j, i, a, b]), do_all, NN).astype(BF).reshape(shape)
            return carry

        lax.fori_loop(0, GRID, column, 0)
        one, two, three = (turn(sw, d, GRID) for d in (1, 2, 3))
        made = (
            sems.copy(dkp[j].at[two], relk.at[j], after),
            sems.copy(dvp[j].at[two], relv.at[j], before),
            sems.copy(dkp[j].at[three], nearkv.at[0, j], before),
            sems.copy(dvp[j].at[one], nearkv.at[1, j], after),
        )
        done.extend(made)
        rs_first.append(made)

    def combine(j):
        take(rs_first[j][:2])
        one, three = turn(sw, 1, GRID), turn(sw, 3, GRID)
        cmbk[j] = (relk[j].astype(F32) + dkp[j][one].astype(F32)).astype(BF)
        cmbv[j] = (relv[j].astype(F32) + dvp[j][three].astype(F32)).astype(BF)
        made = (
            sems.copy(cmbk.at[j], farkv.at[0, j], after),
            sems.copy(cmbv.at[j], farkv.at[1, j], before),
        )
        done.extend(made)
        rs_second.append(made)

    def finish(j):
        take(rs_first[j][2:])
        take(rs_second[j])
        for n, (own, total, there) in enumerate(((dkp, sumk, dkh), (dvp, sumv, dvh))):
            total[j] = (
                own[j][sw].astype(F32) + nearkv[n, j].astype(F32) + farkv[n, j].astype(F32)
            ).astype(BF)
            there[sh * GROUP + j] = total[j, sh]
            made = [sems.copy(total.at[j, p[1]], there.at[sh * GROUP + j], p) for p in row_peer]
            done.extend(made)
            back_got.extend(made)

    backward(0)
    backward(1)
    combine(0)
    backward(2)
    combine(1)

    take(o_got)
    for h in range(HEADS):
        rows[:, h * HEAD : (h + 1) * HEAD] = oh[h]
    lora = dot(rows[...], downt[...], NT).astype(BF)
    ad[pl.ds(0, RANK), :] = dot(mid[...], rows[...], TN).astype(BF)
    ad[pl.ds(RANK, RANK), :] = dot(lora, og[...], TN).astype(BF)
    part = 2 * RANK // GRID

    def strip(owner):
        return pl.ds(pl.multiple_of(owner * part, part), part)

    y_got = [sems.copy(ad.at[strip(p[2])], ry.at[n], p) for n, p in enumerate(col_peer)]
    finish(0)
    combine(2)
    for n in range(GRID):
        block = slice(n * SPAN, (n + 1) * SPAN)
        out[:, block] = (
            dot(rows[...], wt[block, :], NT) + dot(lora, up[:, block], NN)
        ).astype(BF)

    take(y_got)
    summed = ad[strip(sw), :].astype(F32)
    for n in range(3):
        summed = summed + ry[n].astype(F32)
    for n in range(GRID):
        zsrc[n] = summed[:, n * SPAN : (n + 1) * SPAN].astype(BF)
    z_got = [sems.copy(zsrc.at[p[1]], rz.at[n], p) for n, p in enumerate(row_peer)]
    finish(1)

    take(z_got)
    summed = zsrc[sh].astype(F32)
    for n in range(3):
        summed = summed + rz[n].astype(F32)
    dpsrc[...] = summed.astype(BF)
    rdp[dp] = dpsrc[...]
    d_got = [sems.copy(dpsrc, rdp.at[dp], p) for p in dp_peer]
    finish(2)

    take(dq_got)
    for h in range(HEADS):
        dq_out[:, h * HEAD : (h + 1) * HEAD] = dqh[h]

    take(d_got)
    summed = rdp[0].astype(F32)
    for n in range(1, 16):
        summed = summed + rdp[n].astype(F32)
    full[sw, sh] = summed.astype(BF)
    spot = full.at[sw, sh]
    g_got = [sems.copy(spot, spot, p) for p in row_peer]
    take(g_got)
    spot = full.at[sw]
    h_got = [sems.copy(spot, spot, p) for p in col_peer]

    take(back_got)
    for h in range(HEADS):
        dk_out[:, h * HEAD : (h + 1) * HEAD] = dkh[h]
        dv_out[:, h * HEAD : (h + 1) * HEAD] = dvh[h]
    take(h_got)
    norm = TOKENS ** (-0.5)
    for c in range(GRID):
        for r in range(GRID):
            grads[c * part : (c + 1) * part, r * SPAN : (r + 1) * SPAN] = (
                full[c, r].astype(F32) * norm
            )
    for made in done + y_got + z_got + d_got + g_got + h_got:
        made.wait_send()


VM = pl.BlockSpec(memory_space=pltpu.VMEM)
SM = pl.BlockSpec(memory_space=pltpu.SMEM)
ANY = pl.BlockSpec(memory_space=pl.ANY)


def shaped(*dims, kind=BF):
    return jax.ShapeDtypeStruct(dims, kind)


def body(query, key, value, first_tile, weight, down, up, out_grad):
    shape = query.shape
    q, k, v, og = (a.reshape(TOK, FEAT) for a in (query, key, value, out_grad))
    dma = pltpu.SemaphoreType.DMA
    flat = (TOK, FEAT)
    part = 2 * RANK // GRID
    tiles = (GRID, TOK, HEAD)

    def buf(*dims, kind=BF):
        return pltpu.VMEM(dims, kind)

    def each(*dims):
        return [buf(*dims) for _ in range(GROUP)]

    output, dq, dk, dv, grads = pl.pallas_call(
        kernel,
        name="attend",
        out_shape=(
            shaped(*flat), shaped(*flat), shaped(*flat), shaped(*flat),
            shaped(2 * RANK, FEAT, kind=F32),
        ),
        in_specs=[SM] + [ANY] * 7,
        out_specs=[VM] * 5,
        scratch_shapes=[
            buf(*flat), buf(*flat), buf(*flat), buf(*flat), buf(SHARD, FEAT), buf(RANK, FEAT), buf(RANK, FEAT),
            buf(HEADS, TOK, HEAD), buf(HEADS, TOK, HEAD), buf(HEADS, TOK, HEAD), buf(HEADS, TOK, HEAD),
            buf(FEAT, FEAT), buf(TOK, RANK),
            each(GRID, *tiles), each(GRID, *tiles), each(*tiles), each(*tiles),
            buf(GROUP, GRID, WINDOW, WINDOW, TOK, TOK), buf(GROUP, GRID, HEAD, TOK, kind=F32),
            buf(GRID, WINDOW, WINDOW, TOK, TOK), each(*tiles), each(*tiles),
            each(GRID, *tiles), each(GRID, *tiles),
            buf(GROUP, *tiles), buf(GROUP, *tiles), buf(GROUP, *tiles), buf(GROUP, *tiles),
            buf(2, GROUP, *tiles), buf(2, GROUP, *tiles), buf(GROUP, *tiles), buf(GROUP, *tiles),
            buf(HEADS, TOK, HEAD), buf(HEADS, TOK, HEAD), buf(HEADS, TOK, HEAD), buf(HEADS, TOK, HEAD),
            buf(*flat), buf(2 * RANK, FEAT), buf(3, part, FEAT), buf(GRID, part, SPAN),
            buf(3, part, SPAN), buf(part, SPAN), buf(16, part, SPAN), buf(GRID, GRID, part, SPAN),
            dma((7,)), dma((COPIES,)), dma((COPIES,)),
        ],
        compiler_params=pltpu.CompilerParams(
            collective_id=0, has_side_effects=True, vmem_limit_bytes=56 << 20
        ),
    )(first_tile, q, k, v, og, weight.T, down.T, up)
    return (
        output.reshape(shape),
        dq.reshape(shape),
        dk.reshape(shape),
        dv.reshape(shape),
        grads[:RANK].T,
        grads[RANK:],
    )


def solution(mesh):
    tiles = P("dp", None, "sh", "sw", None)
    return jax.shard_map(
        body,
        mesh=mesh,
        in_specs=(tiles, tiles, tiles, P(), P(None, "dp"), P(), P(), tiles),
        out_specs=(tiles, tiles, tiles, tiles, P(), P()),
        check_vma=False,
    )
```

time: 186 us -> 132 us (0.71); the launches traced: 186 us -> 130 us
  Pallas kernels: 170 us -> 123 us
  local copies, waits for them, and re-layouts: 15.1 us -> 6.26 us
    pallas_call x3 -> x1, Pallas kernels: 170 us -> 123 us  [body(): pl.pallas_call(kernel, name='attend', out_shape=(shaped(*flat), shaped(*f...]
    unnamed x32 -> x12, local copies, waits for them, and re-layouts: 14 us -> 4.16 us
where the time goes in v2:
time: 132 us; the launch traced here: 130 us
  Pallas kernels  123 us (93%)
  local copies, waits for them, and re-layouts  6.26 us (5%)
    pallas_call x1, Pallas kernels, body(): pl.pallas_call(kernel, name='attend', out_shape=(shaped(*flat), shaped(*f...  123 us
    unnamed x12, local copies, waits for them, and re-layouts  4.16 us

profile of v2, /device:TPU:32, one launch (start us, length us, event | category | flops | bytes accessed | tf_op | source)
XLA Modules:
  0.0 130.2 jit_solution(11715344930629313017)
XLA Ops:
  0.6 123.3 %attend.1 = (bf16[128,1536]{1,0:T(8,128)(2,1)}, bf16[128,1536]{1,0:T(8,128)(2,1)}, bf16[128,1536]{1,0:T(8,128)(2,1)}, bf16[128,1536]{1,0:T(8,128)(2,1)}, f32[128,1536]{1,0:T(8,128)}) custom-call(s32[2,4,4]{2,1,0:T(4,128)} %table.1, bf16[128,1536]{1,0:T(8,128)(2,1)} %bitcast.16, bf16[128,1536]{1,0:T(8,128)(2,1)} %bitcast.17, bf16[128,1536]{1,0:T(8,128)(2,1)} %bitcast.18, ...), custom_call_target="tpu_custom_call" | custom-call | tf_op jit(solution)/shard_map/attend/pallas_call | solution.py:445
  123.9 0.0 copy-start.3
  123.9 2.1 %fusion = (f32[64,1536]{1,0:T(8,128)}, f32[1536,64]{0,1:T(8,128)}) fusion(f32[128,1536]{1,0:T(8,128)} %get-tuple-element.15), kind=kLoop, calls=%fused_computation.1 | loop fusion | bytes 1572864 | tf_op jit(solution)/shard_map/slice | solution.py:479
  126.0 0.0 copy-done.3
  126.0 0.0 copy-start.2
  126.0 0.7 copy.18
  126.8 0.4 copy-done.2
  127.2 0.0 copy-start.1
  127.2 0.7 copy.19
  127.9 0.4 copy-done.1
  128.3 0.0 copy-start
  128.3 0.7 copy.20
  129.1 0.4 copy-done
  129.5 0.7 copy.21
Async XLA Ops:
  123.9 2.1 %copy-start.3 = (bf16[128,1536]{1,0:T(8,128)(2,1)S(1)}, bf16[128,1536]{1,0:T(8,128)(2,1)}, u32[]{:S(2)}) copy-start(bf16[128,1536]{1,0:T(8,128)(2,1)} %get-tuple-element.11) | copy-start | bytes 1179652
  126.0 1.1 copy-start.2
  127.2 1.1 copy-start.1
  128.3 1.1 copy-start

commit v3 on v2

--- a/solution.py
+++ b/solution.py
@@ -61,18 +61,19 @@
     return dp + bit - 2 * bit * lax.rem(lax.div(dp, bit), 2)
 
 
-COPIES = 15 + 36 + 18 + 18 + 36 + 27
+COPIES = 16 + 36 + 18 + 18 + 36 + 27
 
 
 def kernel(
     table, q_hbm, k_hbm, v_hbm, og_hbm, w_hbm, down_hbm, up_hbm,
-    out, dq_out, dk_out, dv_out, grads,
+    out_hbm, dq_hbm, dk_hbm, dv_hbm, down_grad_hbm, up_grad_hbm,
+    out, dq_out, dk_out, dv_out, down_grad, up_grad,
     q_in, k_in, v_in, og, w_in, downt, up,
     qs, ks, vs, dos, wt, mid,
     kj, vj, qj, doj, prob, att, dsl, oj, dqj, dkp, dvp,
     relk, relv, cmbk, cmbv, nearkv, farkv, sumk, sumv,
     oh, dqh, dkh, dvh, rows, ad, ry, zsrc, rz, dpsrc, rdp, full,
-    local, send, recv,
+    local, storing, send, recv,
 ):
     dp, sh, sw = place()
     sems = Sems(send, recv)
@@ -84,8 +85,10 @@
     east, west = dp_peer[3], dp_peer[11]
     mate = flip(dp, 2)
     zlo = (mate, sh, sw)
+    low = lax.rem(lax.div(dp, 2), 2)
+    zlo_over = (mate, turn(sh, 3 + 2 * low, GRID), sw)
     twin = (flip(dp, 1), sh, sw)
-    peers = row_peer + col_peer + dp_peer
+    peers = row_peer + col_peer + dp_peer + [zlo_over]
 
     loads = []
     for n, (src, dst) in enumerate(
@@ -101,6 +104,10 @@
     def shard_of(owner):
         return wt.at[pl.ds(pl.multiple_of(owner * SHARD, SHARD), SHARD)]
 
+    def half_of(owner, n):
+        start = pl.multiple_of(owner * SHARD + n * (SHARD // 2), SHARD // 2)
+        return wt.at[pl.ds(start, SHARD // 2)]
+
     def pass_on(owner, peer):
         return sems.copy(shard_of(owner), shard_of(owner), peer)
 
@@ -129,7 +136,9 @@
         return scatter(ks, kj[j].at[sw, sh], j) + scatter(vs, vj[j].at[sw, sh], j)
 
     kv = [send_kv(0)]
-    mate_in = pass_on(dp, zlo)
+    mate_in = [
+        sems.copy(half_of(dp, n), half_of(dp, n), peer) for n, peer in enumerate((zlo, zlo_over))
+    ]
     own_east, own_west = pass_on(dp, east), pass_on(dp, west)
     twin_in = [pass_on(dp, twin)]
     for j in range(GROUP):
@@ -145,10 +154,6 @@
         qj[j][sh] = qs[sh * GROUP + j]
     loads[6].wait()
 
-    mate_in.wait_recv()
-    mate_east, mate_west = pass_on(mate, east), pass_on(mate, west)
-    twin_in.append(pass_on(mate, twin))
-
     near, relay = [], []
 
     def spread_near(j):
@@ -174,37 +179,37 @@
         )
         done.extend(relay[j])
 
-    spread_near(0)
-    kv.append(send_kv(1))
-    q_got = [scatter(qs, qj[0].at[sh], 0)]
-
     def owner_at(step):
         return turn(dp, step, 16)
 
+    kv.append(send_kv(1))
+    take(mate_in)
+    mate_east, mate_west = pass_on(mate, east), pass_on(mate, west)
+    twin_in.append(pass_on(mate, twin))
+    spread_near(0)
+    q_got = [scatter(qs, qj[0].at[sh], 0)]
+    kv.append(send_kv(2))
     own_east.wait_recv()
     own_far = pass_on(owner_at(12), east)
     twin_in.append(pass_on(owner_at(12), twin))
     own_west.wait_recv()
     twin_in.append(pass_on(owner_at(4), twin))
-
     spread_far(0)
+    spread_near(1)
+    q_got.append(scatter(qs, qj[1].at[sh], 1))
+    q_got.append(scatter(qs, qj[2].at[sh], 2))
     mate_west.wait_recv()
     mate_far = pass_on(flip(owner_at(4), 2), west)
     twin_in.append(pass_on(flip(owner_at(4), 2), twin))
     mate_east.wait_recv()
     twin_in.append(pass_on(flip(owner_at(12), 2), twin))
-
-    spread_near(1)
-    kv.append(send_kv(2))
-    spread_far(1)
     own_far.wait_recv()
     twin_in.append(pass_on(owner_at(8), twin))
     mate_far.wait_recv()
     twin_in.append(pass_on(flip(owner_at(8), 2), twin))
-    done.extend(twin_in + [mate_in, own_east, own_west, mate_east, mate_west, own_far, mate_far])
+    spread_far(1)
     spread_near(2)
-    q_got.append(scatter(qs, qj[1].at[sh], 1))
-    q_got.append(scatter(qs, qj[2].at[sh], 2))
+    done.extend(twin_in + mate_in + [own_east, own_west, mate_east, mate_west, own_far, mate_far])
 
     def window(stack, i, c):
         row, col = table[0, i, sw], table[1, i, sw]
@@ -255,15 +260,11 @@
                     dos[target * GROUP + j] = piece
                 else:
                     doj[j][sh] = piece
-        for j in range(GROUP):
-            made[j] = scatter(dos, doj[j].at[sh], j)
+            if d:
+                peer = (dp, target, sw)
+                made[0].append(sems.copy(dos.at[target * GROUP], doj[0].at[sh], peer))
+        done.extend(made[0])
         return made
-
-    do_got = project_back()
-    spread_far(2)
-    forward(0)
-    forward(1)
-    forward(2)
 
     dq_got, rs_first, rs_second, back_got = [], [], [], []
 
@@ -283,16 +284,12 @@
             dqj[j][i] = dq.T.astype(BF)
             return carry
 
-        lax.fori_loop(0, GRID, unit, 0)
-        dqh[sh * GROUP + j] = dqj[j][sh]
-        made = [sems.copy(dqj[j].at[p[1]], dqh.at[sh * GROUP + j], p) for p in row_peer]
-        done.extend(made)
-        dq_got.extend(made)
         q_all = qj[j][...].reshape(GRID * TOK, HEAD)
         do_all = doj[j][...].reshape(GRID * TOK, HEAD)
-
-        def column(c, carry):
-            def gathered(load):
+        one, two, three = (turn(sw, d, GRID) for d in (1, 2, 3))
+
+        def sum_columns(load, other, total):
+            def column(c, carry):
                 lines = []
                 for r in range(GRID):
                     blocks = []
@@ -303,23 +300,25 @@
                         block = load(i, jnp.clip(cc, 0, WINDOW - 1), jnp.clip(rr, 0, WINDOW - 1))
                         blocks.append(jnp.where(inside, block, jnp.zeros_like(block)))
                     lines.append(jnp.concatenate(blocks, axis=1))
-                return jnp.concatenate(lines, axis=0)
-
-            shape = (GRID, TOK, HEAD)
-            dkp[j][c] = dot(gathered(lambda i, a, b: dsl[i, a, b]), q_all, NN).astype(BF).reshape(shape)
-            dvp[j][c] = dot(gathered(lambda i, a, b: prob[j, i, a, b]), do_all, NN).astype(BF).reshape(shape)
-            return carry
-
-        lax.fori_loop(0, GRID, column, 0)
-        one, two, three = (turn(sw, d, GRID) for d in (1, 2, 3))
-        made = (
-            sems.copy(dkp[j].at[two], relk.at[j], after),
-            sems.copy(dvp[j].at[two], relv.at[j], before),
-            sems.copy(dkp[j].at[three], nearkv.at[0, j], before),
-            sems.copy(dvp[j].at[one], nearkv.at[1, j], after),
-        )
+                lines = jnp.concatenate(lines, axis=0)
+                total[c] = dot(lines, other, NN).astype(BF).reshape(GRID, TOK, HEAD)
+                return carry
+
+            lax.fori_loop(0, GRID, column, 0)
+
+        sum_columns(lambda i, a, b: prob[j, i, a, b], do_all, dvp[j])
+        v_far = sems.copy(dvp[j].at[two], relv.at[j], before)
+        v_near = sems.copy(dvp[j].at[one], nearkv.at[1, j], after)
+        lax.fori_loop(0, GRID, unit, 0)
+        sum_columns(lambda i, a, b: dsl[i, a, b], q_all, dkp[j])
+        k_far = sems.copy(dkp[j].at[two], relk.at[j], after)
+        k_near = sems.copy(dkp[j].at[three], nearkv.at[0, j], before)
+        rs_first.append((k_far, v_far, k_near, v_near))
+        done.extend(rs_first[j])
+        dqh[sh * GROUP + j] = dqj[j][sh]
+        made = [sems.copy(dqj[j].at[p[1]], dqh.at[sh * GROUP + j], p) for p in row_peer]
         done.extend(made)
-        rs_first.append(made)
+        dq_got.extend(made)
 
     def combine(j):
         take(rs_first[j][:2])
@@ -345,11 +344,33 @@
             done.extend(made)
             back_got.extend(made)
 
+    part = 2 * RANK // GRID
+
+    def strip(owner):
+        return pl.ds(pl.multiple_of(owner * part, part), part)
+
+    def write_out(n, src, dst):
+        made = pltpu.make_async_copy(src, dst, storing.at[n])
+        made.start()
+        return made
+
+    def project(blocks):
+        for n in blocks:
+            block = slice(n * SPAN, (n + 1) * SPAN)
+            out[:, block] = (
+                dot(rows[...], wt[block, :], NT) + dot(lora, up[:, block], NN)
+            ).astype(BF)
+
+    forward(0)
+    do_got = project_back()
+    forward(1)
+    spread_far(2)
+    do_got[1] = scatter(dos, doj[1].at[sh], 1)
     backward(0)
+    do_got[2] = scatter(dos, doj[2].at[sh], 2)
+    forward(2)
     backward(1)
     combine(0)
-    backward(2)
-    combine(1)
 
     take(o_got)
     for h in range(HEADS):
@@ -357,19 +378,9 @@
     lora = dot(rows[...], downt[...], NT).astype(BF)
     ad[pl.ds(0, RANK), :] = dot(mid[...], rows[...], TN).astype(BF)
     ad[pl.ds(RANK, RANK), :] = dot(lora, og[...], TN).astype(BF)
-    part = 2 * RANK // GRID
-
-    def strip(owner):
-        return pl.ds(pl.multiple_of(owner * part, part), part)
-
     y_got = [sems.copy(ad.at[strip(p[2])], ry.at[n], p) for n, p in enumerate(col_peer)]
-    finish(0)
-    combine(2)
-    for n in range(GRID):
-        block = slice(n * SPAN, (n + 1) * SPAN)
-        out[:, block] = (
-            dot(rows[...], wt[block, :], NT) + dot(lora, up[:, block], NN)
-        ).astype(BF)
+    backward(2)
+    combine(1)
 
     take(y_got)
     summed = ad[strip(sw), :].astype(F32)
@@ -378,7 +389,8 @@
     for n in range(GRID):
         zsrc[n] = summed[:, n * SPAN : (n + 1) * SPAN].astype(BF)
     z_got = [sems.copy(zsrc.at[p[1]], rz.at[n], p) for n, p in enumerate(row_peer)]
-    finish(1)
+    finish(0)
+    project((0, 1))
 
     take(z_got)
     summed = zsrc[sh].astype(F32)
@@ -387,11 +399,10 @@
     dpsrc[...] = summed.astype(BF)
     rdp[dp] = dpsrc[...]
     d_got = [sems.copy(dpsrc, rdp.at[dp], p) for p in dp_peer]
-    finish(2)
-
-    take(dq_got)
-    for h in range(HEADS):
-        dq_out[:, h * HEAD : (h + 1) * HEAD] = dqh[h]
+    combine(2)
+    finish(1)
+    project((2, 3))
+    stores = [write_out(0, out, out_hbm)]
 
     take(d_got)
     summed = rdp[0].astype(F32)
@@ -400,26 +411,53 @@
     full[sw, sh] = summed.astype(BF)
     spot = full.at[sw, sh]
     g_got = [sems.copy(spot, spot, p) for p in row_peer]
+    finish(2)
+
     take(g_got)
     spot = full.at[sw]
     h_got = [sems.copy(spot, spot, p) for p in col_peer]
+    take(dq_got)
+    for h in range(HEADS):
+        dq_out[:, h * HEAD : (h + 1) * HEAD] = dqh[h]
+    stores.append(write_out(1, dq_out, dq_hbm))
+
+    take(h_got)
+    norm = TOKENS ** (-0.5)
+    for c in range(GRID):
+        half = down_grad if c < GRID // 2 else up_grad
+        start = (c % (GRID // 2)) * part
+        for r in range(GRID):
+            half[start : start + part, r * SPAN : (r + 1) * SPAN] = full[c, r].astype(F32) * norm
+    stores.append(write_out(2, down_grad, down_grad_hbm))
+    stores.append(write_out(3, up_grad, up_grad_hbm))
 
     take(back_got)
     for h in range(HEADS):
         dk_out[:, h * HEAD : (h + 1) * HEAD] = dkh[h]
         dv_out[:, h * HEAD : (h + 1) * HEAD] = dvh[h]
-    take(h_got)
-    norm = TOKENS ** (-0.5)
-    for c in range(GRID):
-        for r in range(GRID):
-            grads[c * part : (c + 1) * part, r * SPAN : (r + 1) * SPAN] = (
-                full[c, r].astype(F32) * norm
-            )
+    stores.append(write_out(4, dk_out, dk_hbm))
+    stores.append(write_out(5, dv_out, dv_hbm))
     for made in done + y_got + z_got + d_got + g_got + h_got:
         made.wait_send()
-
-
-VM = pl.BlockSpec(memory_space=pltpu.VMEM)
+    for made in stores:
+        made.wait()
+
+
+def finish_kernel(*refs):
+    count = len(refs) // 3
+    sems = refs[-1]
+    here = refs[2 * count : 3 * count]
+    reads = [pltpu.make_async_copy(refs[n], here[n], sems.at[0, n]) for n in range(count)]
+    writes = [pltpu.make_async_copy(here[n], refs[count + n], sems.at[1, n]) for n in range(count)]
+    for copy in reads:
+        copy.start()
+    for n in range(count):
+        reads[n].wait()
+        writes[n].start()
+    for copy in writes:
+        copy.wait()
+
+
 SM = pl.BlockSpec(memory_space=pltpu.SMEM)
 ANY = pl.BlockSpec(memory_space=pl.ANY)
 
@@ -442,16 +480,18 @@
     def each(*dims):
         return [buf(*dims) for _ in range(GROUP)]
 
-    output, dq, dk, dv, grads = pl.pallas_call(
+    results = (
+        shaped(*flat), shaped(*flat), shaped(*flat), shaped(*flat),
+        shaped(RANK, FEAT, kind=F32), shaped(RANK, FEAT, kind=F32),
+    )
+    made = pl.pallas_call(
         kernel,
         name="attend",
-        out_shape=(
-            shaped(*flat), shaped(*flat), shaped(*flat), shaped(*flat),
-            shaped(2 * RANK, FEAT, kind=F32),
-        ),
+        out_shape=results,
         in_specs=[SM] + [ANY] * 7,
-        out_specs=[VM] * 5,
+        out_specs=[ANY] * 6,
         scratch_shapes=[
+            buf(*flat), buf(*flat), buf(*flat), buf(*flat), buf(RANK, FEAT, kind=F32), buf(RANK, FEAT, kind=F32),
             buf(*flat), buf(*flat), buf(*flat), buf(*flat), buf(SHARD, FEAT), buf(RANK, FEAT), buf(RANK, FEAT),
             buf(HEADS, TOK, HEAD), buf(HEADS, TOK, HEAD), buf(HEADS, TOK, HEAD), buf(HEADS, TOK, HEAD),
             buf(FEAT, FEAT), buf(TOK, RANK),
@@ -464,19 +504,27 @@
             buf(HEADS, TOK, HEAD), buf(HEADS, TOK, HEAD), buf(HEADS, TOK, HEAD), buf(HEADS, TOK, HEAD),
             buf(*flat), buf(2 * RANK, FEAT), buf(3, part, FEAT), buf(GRID, part, SPAN),
             buf(3, part, SPAN), buf(part, SPAN), buf(16, part, SPAN), buf(GRID, GRID, part, SPAN),
-            dma((7,)), dma((COPIES,)), dma((COPIES,)),
+            dma((7,)), dma((6,)), dma((COPIES,)), dma((COPIES,)),
         ],
         compiler_params=pltpu.CompilerParams(
             collective_id=0, has_side_effects=True, vmem_limit_bytes=56 << 20
         ),
     )(first_tile, q, k, v, og, weight.T, down.T, up)
+    output, dq, dk, dv, down_grad, up_grad = pl.pallas_call(
+        finish_kernel,
+        name="finish",
+        out_shape=results,
+        in_specs=[ANY] * 6,
+        out_specs=[ANY] * 6,
+        scratch_shapes=[pltpu.VMEM(r.shape, r.dtype) for r in results] + [dma((2, 6))],
+    )(*made)
     return (
         output.reshape(shape),
         dq.reshape(shape),
         dk.reshape(shape),
         dv.reshape(shape),
-        grads[:RANK].T,
-        grads[RANK:],
+        down_grad.T,
+        up_grad,
     )
 
 

time: 132 us -> 112 us (0.85); the launches traced: 130 us -> 112 us
  Pallas kernels: 123 us -> 112 us
  local copies, waits for them, and re-layouts: 6.26 us -> 0 us
    pallas_call x1 -> x2, Pallas kernels: 123 us -> 112 us  [the longest x1 109 us: body(): pl.pallas_call(kernel, name='attend', out_shape=results, in_specs=[SM] +...]
    unnamed x12 -> x0, local copies, waits for them, and re-layouts: 4.16 us -> none
    slice x1 -> x0, local copies, waits for them, and re-layouts: 2.1 us -> none  [body(): grads[RANK:]]
where the time goes in v3:
time: 112 us
  Pallas kernels  112 us (100%)
    pallas_call x1, Pallas kernels, body(): pl.pallas_call(kernel, name='attend', out_shape=results, in_specs=[SM] +...  109 us
    pallas_call x1, Pallas kernels, body(): pl.pallas_call(finish_kernel, name='finish', out_shape=results, in_specs=...  2.49 us

profile of v3, /device:TPU:32, one launch (start us, length us, event | category | flops | bytes accessed | tf_op | source)
XLA Modules:
  0.0 112.2 jit_solution(16528439339689855735)
XLA Ops:
  0.6 109.0 %attend.1 = (bf16[128,1536]{1,0:T(8,128)(2,1)}, bf16[128,1536]{1,0:T(8,128)(2,1)}, bf16[128,1536]{1,0:T(8,128)(2,1)}, bf16[128,1536]{1,0:T(8,128)(2,1)}, f32[64,1536]{1,0:T(8,128)}, /*index=5*/f32[64,1536]{1,0:T(8,128)}) custom-call(s32[2,4,4]{2,1,0:T(4,128)} %table.1, bf16[128,1536]{1,0:T(8,128)(2,1)} %bitcast.11, bf16[128,1536]{1,0:T(8,128)(2,1)} %bitcast.12, ...), custom_call_target="tpu_custom_call" | custom-call | tf_op jit(solution)/shard_map/attend/pallas_call | solution.py:487
  109.7 2.5 %finish.1 = (bf16[128,1536]{1,0:T(8,128)(2,1)}, bf16[128,1536]{1,0:T(8,128)(2,1)}, bf16[128,1536]{1,0:T(8,128)(2,1)}, bf16[128,1536]{1,0:T(8,128)(2,1)}, f32[64,1536]{1,0:T(8,128)}, /*index=5*/f32[64,1536]{1,0:T(8,128)}) custom-call(bf16[128,1536]{1,0:T(8,128)(2,1)} %get-tuple-element.18.refs_0_, bf16[128,1536]{1,0:T(8,128)(2,1)} %get-tuple-element.19.refs_1_, ...), custom_call_target="tpu_custom_call" | custom-call | tf_op jit(solution)/shard_map/finish/pallas_call | solution.py:513

commit v4 on v3

--- a/solution.py
+++ b/solution.py
@@ -66,14 +66,13 @@
 
 def kernel(
     table, q_hbm, k_hbm, v_hbm, og_hbm, w_hbm, down_hbm, up_hbm,
-    out_hbm, dq_hbm, dk_hbm, dv_hbm, down_grad_hbm, up_grad_hbm,
     out, dq_out, dk_out, dv_out, down_grad, up_grad,
     q_in, k_in, v_in, og, w_in, downt, up,
     qs, ks, vs, dos, wt, mid,
     kj, vj, qj, doj, prob, att, dsl, oj, dqj, dkp, dvp,
     relk, relv, cmbk, cmbv, nearkv, farkv, sumk, sumv,
     oh, dqh, dkh, dvh, rows, ad, ry, zsrc, rz, dpsrc, rdp, full,
-    local, storing, send, recv,
+    local, send, recv,
 ):
     dp, sh, sw = place()
     sems = Sems(send, recv)
@@ -127,6 +126,10 @@
         made = [sems.copy(stack.at[p[1] * GROUP + j], dst, p) for p in row_peer]
         done.extend(made)
         return made
+
+    def settle():
+        while done:
+            done.pop().wait_send()
 
     def take(copies):
         for made in copies:
@@ -349,11 +352,6 @@
     def strip(owner):
         return pl.ds(pl.multiple_of(owner * part, part), part)
 
-    def write_out(n, src, dst):
-        made = pltpu.make_async_copy(src, dst, storing.at[n])
-        made.start()
-        return made
-
     def project(blocks):
         for n in blocks:
             block = slice(n * SPAN, (n + 1) * SPAN)
@@ -361,8 +359,8 @@
                 dot(rows[...], wt[block, :], NT) + dot(lora, up[:, block], NN)
             ).astype(BF)
 
+    do_got = project_back()
     forward(0)
-    do_got = project_back()
     forward(1)
     spread_far(2)
     do_got[1] = scatter(dos, doj[1].at[sh], 1)
@@ -402,7 +400,6 @@
     combine(2)
     finish(1)
     project((2, 3))
-    stores = [write_out(0, out, out_hbm)]
 
     take(d_got)
     summed = rdp[0].astype(F32)
@@ -411,6 +408,7 @@
     full[sw, sh] = summed.astype(BF)
     spot = full.at[sw, sh]
     g_got = [sems.copy(spot, spot, p) for p in row_peer]
+    settle()
     finish(2)
 
     take(g_got)
@@ -419,8 +417,8 @@
     take(dq_got)
     for h in range(HEADS):
         dq_out[:, h * HEAD : (h + 1) * HEAD] = dqh[h]
-    stores.append(write_out(1, dq_out, dq_hbm))
-
+
+    settle()
     take(h_got)
     norm = TOKENS ** (-0.5)
     for c in range(GRID):
@@ -428,36 +426,25 @@
         start = (c % (GRID // 2)) * part
         for r in range(GRID):
             half[start : start + part, r * SPAN : (r + 1) * SPAN] = full[c, r].astype(F32) * norm
-    stores.append(write_out(2, down_grad, down_grad_hbm))
-    stores.append(write_out(3, up_grad, up_grad_hbm))
 
     take(back_got)
     for h in range(HEADS):
         dk_out[:, h * HEAD : (h + 1) * HEAD] = dkh[h]
         dv_out[:, h * HEAD : (h + 1) * HEAD] = dvh[h]
-    stores.append(write_out(4, dk_out, dk_hbm))
-    stores.append(write_out(5, dv_out, dv_hbm))
     for made in done + y_got + z_got + d_got + g_got + h_got:
         made.wait_send()
-    for made in stores:
-        made.wait()
 
 
 def finish_kernel(*refs):
-    count = len(refs) // 3
-    sems = refs[-1]
-    here = refs[2 * count : 3 * count]
-    reads = [pltpu.make_async_copy(refs[n], here[n], sems.at[0, n]) for n in range(count)]
-    writes = [pltpu.make_async_copy(here[n], refs[count + n], sems.at[1, n]) for n in range(count)]
-    for copy in reads:
+    count = len(refs) // 2
+    writes = [pltpu.make_async_copy(refs[n], refs[count + n], refs[-1].at[n]) for n in range(count)]
+    for copy in writes:
         copy.start()
-    for n in range(count):
-        reads[n].wait()
-        writes[n].start()
     for copy in writes:
         copy.wait()
 
 
+VM = pl.BlockSpec(memory_space=pltpu.VMEM)
 SM = pl.BlockSpec(memory_space=pltpu.SMEM)
 ANY = pl.BlockSpec(memory_space=pl.ANY)
 
@@ -487,11 +474,10 @@
     made = pl.pallas_call(
         kernel,
         name="attend",
-        out_shape=results,
+        out_shape=tuple(pltpu.VMEM(r.shape, r.dtype) for r in results),
         in_specs=[SM] + [ANY] * 7,
-        out_specs=[ANY] * 6,
+        out_specs=[VM] * 6,
         scratch_shapes=[
-            buf(*flat), buf(*flat), buf(*flat), buf(*flat), buf(RANK, FEAT, kind=F32), buf(RANK, FEAT, kind=F32),
             buf(*flat), buf(*flat), buf(*flat), buf(*flat), buf(SHARD, FEAT), buf(RANK, FEAT), buf(RANK, FEAT),
             buf(HEADS, TOK, HEAD), buf(HEADS, TOK, HEAD), buf(HEADS, TOK, HEAD), buf(HEADS, TOK, HEAD),
             buf(FEAT, FEAT), buf(TOK, RANK),
@@ -504,7 +490,7 @@
             buf(HEADS, TOK, HEAD), buf(HEADS, TOK, HEAD), buf(HEADS, TOK, HEAD), buf(HEADS, TOK, HEAD),
             buf(*flat), buf(2 * RANK, FEAT), buf(3, part, FEAT), buf(GRID, part, SPAN),
             buf(3, part, SPAN), buf(part, SPAN), buf(16, part, SPAN), buf(GRID, GRID, part, SPAN),
-            dma((7,)), dma((6,)), dma((COPIES,)), dma((COPIES,)),
+            dma((7,)), dma((COPIES,)), dma((COPIES,)),
         ],
         compiler_params=pltpu.CompilerParams(
             collective_id=0, has_side_effects=True, vmem_limit_bytes=56 << 20
@@ -514,10 +500,10 @@
         finish_kernel,
         name="finish",
         out_shape=results,
-        in_specs=[ANY] * 6,
+        in_specs=[VM] * 6,
         out_specs=[ANY] * 6,
-        scratch_shapes=[pltpu.VMEM(r.shape, r.dtype) for r in results] + [dma((2, 6))],
-    )(*made)
+        scratch_shapes=[dma((6,))],
+    )(*[pltpu.with_memory_space_constraint(m, pltpu.VMEM) for m in made])
     return (
         output.reshape(shape),
         dq.reshape(shape),

time: 112 us -> 110 us (0.982)
  Pallas kernels: 112 us -> 109 us
    pallas_call x1, Pallas kernels: 109 us -> 107 us  [body(): pl.pallas_call(kernel, name='attend', out_shape=tuple((pltpu.VMEM(r.shape...]
where the time goes in v4:
time: 110 us; the launch traced here: 109 us
  Pallas kernels  109 us (99%)
    pallas_call x1, Pallas kernels, body(): pl.pallas_call(kernel, name='attend', out_shape=tuple((pltpu.VMEM(r.shape...  107 us

profile of v4, /device:TPU:32, one launch (start us, length us, event | category | flops | bytes accessed | tf_op | source)
XLA Modules:
  0.0 109.3 jit_solution(7969578904405078213)
XLA Ops:
  0.6 107.2 %attend.1 = (bf16[128,1536]{1,0:T(8,128)(2,1)S(1)}, bf16[128,1536]{1,0:T(8,128)(2,1)S(1)}, bf16[128,1536]{1,0:T(8,128)(2,1)S(1)}, bf16[128,1536]{1,0:T(8,128)(2,...) custom-call(s32[2,4,4]{2,1,0:T(4,128)} %table.1, bf16[128,1536]{1,0:T(8,128)(2,1)} %bitcast.11, ...), custom_call_target="tpu_custom_call" | custom-call | tf_op jit(solution)/shard_map/attend/pallas_call | solution.py:474
  107.9 1.4 %finish.1 = (bf16[128,1536]{1,0:T(8,128)(2,1)}, bf16[128,1536]{1,0:T(8,128)(2,1)}, bf16[128,1536]{1,0:T(8,128)(2,1)}, bf16[128,1536]{1,0:T(8,128)(2,1)}, f32[64,1536]{1,0:T(8,128)}, /*index=5*/f32[64,1536]{1,0:T(8,128)}) custom-call(bf16[128,1536]{1,0:T(8,128)(2,1)S(1)} %get-tuple-element.18.refs_0_, bf16[128,1536]{1,0:T(8,128)(2,1)S(1)} %get-tuple-element.19.refs_1_, ...), custom_call_target="tpu_custom_call" | custom-call | tf_op jit(solution)/shard_map/finish/pallas_call | solution.py:499

commit v5 on v4

--- a/solution.py
+++ b/solution.py
@@ -114,10 +114,14 @@
     wt[pl.ds(pl.multiple_of(dp * SHARD, SHARD), SHARD), :] = w_in[...]
     loads[1].wait()
     loads[2].wait()
-    for h in range(HEADS):
-        cols = slice(h * HEAD, (h + 1) * HEAD)
-        ks[h] = k_in[:, cols]
-        vs[h] = v_in[:, cols]
+
+    def split_kv(j):
+        for h in range(j, HEADS, GROUP):
+            cols = slice(h * HEAD, (h + 1) * HEAD)
+            ks[h] = k_in[:, cols]
+            vs[h] = v_in[:, cols]
+
+    split_kv(0)
     pl.semaphore_wait(barrier, len(peers))
 
     done = []
@@ -144,6 +148,8 @@
     ]
     own_east, own_west = pass_on(dp, east), pass_on(dp, west)
     twin_in = [pass_on(dp, twin)]
+    split_kv(1)
+    split_kv(2)
     for j in range(GROUP):
         kj[j][sw, sh] = ks[sh * GROUP + j]
         vj[j][sw, sh] = vs[sh * GROUP + j]
@@ -186,12 +192,12 @@
         return turn(dp, step, 16)
 
     kv.append(send_kv(1))
+    kv.append(send_kv(2))
+    q_got = [scatter(qs, qj[j].at[sh], j) for j in range(GROUP)]
     take(mate_in)
     mate_east, mate_west = pass_on(mate, east), pass_on(mate, west)
     twin_in.append(pass_on(mate, twin))
     spread_near(0)
-    q_got = [scatter(qs, qj[0].at[sh], 0)]
-    kv.append(send_kv(2))
     own_east.wait_recv()
     own_far = pass_on(owner_at(12), east)
     twin_in.append(pass_on(owner_at(12), twin))
@@ -199,8 +205,6 @@
     twin_in.append(pass_on(owner_at(4), twin))
     spread_far(0)
     spread_near(1)
-    q_got.append(scatter(qs, qj[1].at[sh], 1))
-    q_got.append(scatter(qs, qj[2].at[sh], 2))
     mate_west.wait_recv()
     mate_far = pass_on(flip(owner_at(4), 2), west)
     twin_in.append(pass_on(flip(owner_at(4), 2), twin))
@@ -361,11 +365,11 @@
 
     do_got = project_back()
     forward(0)
+    do_got[1] = scatter(dos, doj[1].at[sh], 1)
     forward(1)
     spread_far(2)
-    do_got[1] = scatter(dos, doj[1].at[sh], 1)
+    do_got[2] = scatter(dos, doj[2].at[sh], 2)
     backward(0)
-    do_got[2] = scatter(dos, doj[2].at[sh], 2)
     forward(2)
     backward(1)
     combine(0)

time: 110 us -> 110 us (level)
  no operation moved by 1% of the time
where the time goes in v5:
time: 110 us; the launch traced here: 109 us
  Pallas kernels  108 us (98%)
    pallas_call x1, Pallas kernels, body(): pl.pallas_call(kernel, name='attend', out_shape=tuple((pltpu.VMEM(r.shape...  107 us

profile of v5, /device:TPU:32, one launch (start us, length us, event | category | flops | bytes accessed | tf_op | source)
XLA Modules:
  0.0 108.7 jit_solution(2591868641050551474)
XLA Ops:
  0.6 106.6 %attend.1 = (bf16[128,1536]{1,0:T(8,128)(2,1)S(1)}, bf16[128,1536]{1,0:T(8,128)(2,1)S(1)}, bf16[128,1536]{1,0:T(8,128)(2,1)S(1)}, bf16[128,1536]{1,0:T(8,128)(2,...) custom-call(s32[2,4,4]{2,1,0:T(4,128)} %table.1, bf16[128,1536]{1,0:T(8,128)(2,1)} %bitcast.11, ...), custom_call_target="tpu_custom_call" | custom-call | tf_op jit(solution)/shard_map/attend/pallas_call | solution.py:478
  107.3 1.4 %finish.1 = (bf16[128,1536]{1,0:T(8,128)(2,1)}, bf16[128,1536]{1,0:T(8,128)(2,1)}, bf16[128,1536]{1,0:T(8,128)(2,1)}, bf16[128,1536]{1,0:T(8,128)(2,1)}, f32[64,1536]{1,0:T(8,128)}, /*index=5*/f32[64,1536]{1,0:T(8,128)}) custom-call(bf16[128,1536]{1,0:T(8,128)(2,1)S(1)} %get-tuple-element.18.refs_0_, bf16[128,1536]{1,0:T(8,128)(2,1)S(1)} %get-tuple-element.19.refs_1_, ...), custom_call_target="tpu_custom_call" | custom-call | tf_op jit(solution)/shard_map/finish/pallas_call | solution.py:503
